TPU v7x, 256 devices: a whole 4x4x8 slice. The times are simulated.
256 devices in a mesh: fsdp: 64 (over x, z, core), rep: 4 (over y).
Axes of the slice: x: 4, y: 4, z: 8, core: 2. Of those that a mesh axis runs over, the one named last changes fastest.
Arguments:
- grads: bfloat16 [2, 16, 512, 6144], P(None, None, 'fsdp', 'rep'), may hold values from -8 to 8
- second_moment: float32 [2, 16, 512, 6144], P(None, None, 'fsdp', 'rep'), may hold values from 0.015 to 10, as said below
- momentum: float32 [2, 16, 512, 6144], P(None, None, 'fsdp', 'rep'), may hold values from -6 to 6
- left_inverse_root: float32 [4, 64, 3, 512, 512], P('rep', 'fsdp'), may hold values from -1 to 6, as said below
- right_root: float32 [4, 64, 3, 512, 512], P('rep', 'fsdp'), may hold values from -1 to 6, as said below
- owner: int32 [4, 96], P('rep'), may hold values from 0 to 63, as said below
- slot: int32 [4, 96], P('rep'), may hold values from 0 to 2, as said below
Outputs:
- moment_new: float32 [2, 16, 512, 6144], P(None, None, 'fsdp', 'rep')
- momentum_new: float32 [2, 16, 512, 6144], P(None, None, 'fsdp', 'rep')
Inputs may be any that keep to these rules, and one draw needn't show every extreme that they name: Within one rep index no two blocks share an (owner, slot) pair, and some owner holds 3 blocks. `slot`: slots of the blocks at their owners, as described for owner. `left_inverse_root`: symmetric factors. `right_root`: symmetric factors. `second_moment`: positive second moments.
All inputs are finite; a program needn't handle non-finite values.
Results may differ from a plain program's by a relative error of at most 0.0003.
Values may be sent and summed in bfloat16 or wider, within the bound.
A program may use at most 64 MiB of HBM per device.

v0:
```python
import jax
import jax.numpy as jnp
from jax import lax
from jax.sharding import PartitionSpec as P


def products(tile_blocks, lefts, rights):
    inner_prod = jnp.einsum("sij,sjk->sik", tile_blocks, rights, precision=lax.Precision.HIGHEST)
    return jnp.einsum("sij,sjk->sik", lefts, inner_prod, precision=lax.Precision.HIGHEST)


def shards(grads, second_moment, momentum, left_inverse_root, right_root, owner, slot):
    sharded_data_count = lax.axis_size("fsdp")
    two, rowblk, rows_per_shard, width = grads.shape
    owner_slot_count = left_inverse_root.shape[2]
    block_item = left_inverse_root.shape[-1]
    colblk = width // block_item
    nblocks = two * rowblk * colblk
    owners = owner[0]
    slots = slot[0]
    g_full = grads.astype(jnp.float32)
    moment_new = 0.9 * second_moment + 0.1 * g_full * g_full
    adam = g_full / (jnp.sqrt(moment_new) + 1e-08)
    adam_part = jnp.sum(adam * adam, axis=(1, 2, 3))
    pieces = grads.reshape(two, rowblk, rows_per_shard, colblk, block_item).transpose(0, 1, 3, 2, 4)
    pieces = pieces.reshape(nblocks, rows_per_shard, block_item)
    target_slot = slots * sharded_data_count + owners
    block_placements = jnp.arange(owner_slot_count * sharded_data_count, dtype=jnp.int32)
    match = target_slot[None, :] == block_placements[:, None]
    block_at = jnp.sum(jnp.where(match, jnp.arange(nblocks, dtype=jnp.int32)[None, :], 0), axis=1)
    filled = jnp.any(match, axis=1)
    outbound_blocks = jnp.where(filled[:, None, None], pieces[block_at], jnp.zeros((), grads.dtype))
    outbound_blocks = outbound_blocks.reshape(
        owner_slot_count, sharded_data_count, rows_per_shard, block_item
    )
    received_blocks = lax.all_to_all(
        outbound_blocks, "fsdp", split_axis=1, concat_axis=1, tiled=True
    )
    tile_blocks = received_blocks.reshape(owner_slot_count, block_item, block_item).astype(
        jnp.float32
    )
    lefts = left_inverse_root[0, 0]
    rights = right_root[0, 0]
    owned_blocks = products(tile_blocks, lefts, rights)
    returned_blocks = lax.all_to_all(
        owned_blocks.reshape(owner_slot_count, sharded_data_count, rows_per_shard, block_item),
        "fsdp",
        split_axis=1,
        concat_axis=1,
        tiled=True,
    )
    flattened_rows = returned_blocks.reshape(
        owner_slot_count * sharded_data_count, rows_per_shard, block_item
    )[target_slot]
    direction = flattened_rows.reshape(two, rowblk, colblk, rows_per_shard, block_item).transpose(
        0, 1, 3, 2, 4
    )
    direction = direction.reshape(two, rowblk, rows_per_shard, width)
    adam_sq = lax.psum(adam_part, ("fsdp", "rep"))
    shampoo_sq = lax.psum(jnp.sum(direction * direction, axis=(1, 2, 3)), ("fsdp", "rep"))
    scale = jnp.sqrt(adam_sq) / (jnp.sqrt(shampoo_sq) + 1e-06)
    momentum_new = 0.9 * momentum + scale[:, None, None, None] * direction
    return (moment_new, momentum_new)


def solution(mesh):
    in_specs = (
        P(None, None, "fsdp", "rep"),
        P(None, None, "fsdp", "rep"),
        P(None, None, "fsdp", "rep"),
        P("rep", "fsdp", None, None, None),
        P("rep", "fsdp", None, None, None),
        P("rep", None),
        P("rep", None),
    )
    out_specs = (P(None, None, "fsdp", "rep"), P(None, None, "fsdp", "rep"))
    return jax.shard_map(shards, mesh=mesh, in_specs=in_specs, out_specs=out_specs, check_vma=False)
```

profile of v0, /device:TPU:1, one launch (start us, length us, event | category | flops | bytes accessed | tf_op | source)
XLA Modules:
  0.0 238.4 jit_solution(8925941847936946670)
XLA Ops:
  0.6 0.0 copy-start
  0.6 0.8 fusion.14
  1.5 0.1 select_reduce_fusion
  1.6 0.1 fusion.12
  1.7 0.1 broadcast_in_dim.33
  1.8 3.2 %gather_fusion = bf16[192,8,512]{2,1,0:T(8,128)(2,1)} fusion(bf16[96,8,512]{2,1,0:T(8,128)(2,1)} %bitcast.39, s32[1024]{0:T(1024)S(1)} %pad_clamp_fusion.1), kind=kCustom, calls=%fused_computation | custom fusion | bytes 3146496 | tf_op jit(solution)/shard_map/gather | solution.py:32
  5.0 1.7 broadcast_select_fusion
  6.7 0.1 copy.15
  6.8 52.6 %all_to_all.10 = bf16[3,64,8,512]{3,2,0,1:T(8,128)(2,1)S(1)} all-to-all(bf16[3,64,8,512]{3,2,0,1:T(8,128)(2,1)S(1)} %copy.15), channel_id=1, replica_groups=mesh['fsdp'=64,'rep'=4] {'fsdp'}, dimensions={1} | all-to-all | bytes 3145728 | tf_op jit(solution)/shard_map/all_to_all | solution.py:36
  59.4 0.0 copy-done
  59.4 0.0 copy-start.1
  59.4 2.8 %fusion.2 = f32[3,512,512]{2,1,0:T(8,128)S(1)} fusion(f32[1,1,3,512,512]{4,3,2,1,0:T(8,128)S(1)} %copy-done, bf16[3,64,8,512]{3,2,0,1:T(8,128)(2,1)S(1)} %all_to_all.10), kind=kOutput, calls=%fused_computation.4 | convolution fusion | flops 4831838208 | bytes 7864320 | tf_op jit(solution)/shard_map/sij,sjk->sik/dot_general | solution.py:8
  62.3 0.0 copy-done.1
  62.3 5.5 %fusion.4 = f32[3,64,8,512]{3,2,1,0:T(8,128)S(1)} fusion(f32[3,512,512]{2,1,0:T(8,128)S(1)} %fusion.2, f32[1,1,3,512,512]{4,3,2,1,0:T(8,128)S(1)} %copy-done.1), kind=kOutput, calls=%fused_computation.8 | convolution fusion | flops 4831838208 | bytes 9437184 | tf_op jit(solution)/shard_map/sij,sjk->sik/dot_general | solution.py:9
  67.8 2.0 copy.17
  69.8 0.0 copy-start.2
  69.8 0.0 copy-start.3
  69.8 6.4 %all-to-all-start.1 = ((f32[3,64,8,512]{3,2,0,1:T(8,128)}), f32[3,64,8,512]{3,2,0,1:T(8,128)}, u32[]{:S(2)}, u32[]{:S(2)}) async-start(f32[3,64,8,512]{3,2,0,1:T(8,128)} %copy.17), calls=%async_computation.1 | async-start | bytes 6291456 | tf_op jit(solution)/shard_map/all_to_all | solution.py:45
  76.2 0.0 copy-done.2
  76.3 0.0 copy-done.3
  76.3 3.7 %fusion.11 = (f32[2]{0:T(128)S(1)}, f32[2,16,8,1536]{3,2,1,0:T(8,128)}) fusion(bf16[2,16,8,1536]{3,2,1,0:T(8,128)(2,1)} %param.7, f32[2,16,8,1536]{3,2,1,0:T(8,128)} %param.8), kind=kLoop, calls=%fused_computation.15 | loop fusion | flops 3538942 | bytes 3932168 | tf_op jit(solution)/shard_map/reduce_sum | solution.py:24
  79.9 69.7 %all-to-all-done.1 = f32[3,64,8,512]{3,2,0,1:T(8,128)} async-done(((f32[3,64,8,512]{3,2,0,1:T(8,128)}), f32[3,64,8,512]{3,2,0,1:T(8,128)}, u32[]{:S(2)}, u32[]{:S(2)}) %all-to-all-start.1) | async-done | bytes 3145760 | tf_op jit(solution)/shard_map/all_to_all | solution.py:45
  149.7 4.0 %copy.18 = f32[3,64,8,512]{3,2,1,0:T(8,128)} copy(f32[3,64,8,512]{3,2,0,1:T(8,128)} %all-to-all-done.1) | data formatting | bytes 6291456 | tf_op jit(solution)/shard_map/all_to_all | solution.py:45
  153.7 3.7 %gather_fusion.1 = f32[96,8,512]{2,1,0:T(8,128)} fusion(f32[192,8,512]{2,1,0:T(8,128)} %bitcast.38, s32[1024]{0:T(1024)S(1)} %pad_clamp_fusion), kind=kCustom, calls=%fused_computation.1 | custom fusion | bytes 3146112 | tf_op jit(solution)/shard_map/gather | solution.py:52
  157.3 1.7 multiply_reduce_fusion
  159.0 76.0 %all-reduce = (f32[2]{0:T(128)S(1)}, f32[2]{0:T(128)S(1)}) all-reduce(f32[2]{0:T(128)S(1)} %multiply_reduce_fusion, f32[2]{0:T(128)S(1)} %get-tuple-element.4), channel_id=1, replica_groups=mesh['fsdp'=64,'rep'=4] {'fsdp','rep'}, use_global_device_ids=true, to_apply=%region_5.6 | all-reduce | flops 4 | bytes 32 | tf_op jit(solution)/shard_map/psum | solution.py:60
  235.0 3.4 %multiply_add_fusion = f32[2,16,8,1536]{3,2,1,0:T(8,128)} fusion(f32[2,16,8,1536]{3,2,1,0:T(8,128)} %bitcast.37, f32[2,16,8,1536]{3,2,1,0:T(8,128)} %param.9, f32[2]{0:T(128)S(1)} %add_divide_fusion), kind=kLoop, calls=%fused_computation.13 | loop fusion | flops 1179648 | bytes 4718600 | tf_op jit(solution)/shard_map/add | solution.py:62
  (5 shorter events, 0.0 us)
Async XLA Ops:
  0.6 58.8 %copy-start = (f32[1,1,3,512,512]{4,3,2,1,0:T(8,128)S(1)}, f32[1,1,3,512,512]{4,3,2,1,0:T(8,128)}, u32[]{:S(2)}) copy-start(f32[1,1,3,512,512]{4,3,2,1,0:T(8,128)} %param.11) | copy-start | bytes 9437188
  59.4 2.9 %copy-start.1 = (f32[1,1,3,512,512]{4,3,2,1,0:T(8,128)S(1)}, f32[1,1,3,512,512]{4,3,2,1,0:T(8,128)}, u32[]{:S(2)}) copy-start(f32[1,1,3,512,512]{4,3,2,1,0:T(8,128)} %param.10) | copy-start | bytes 9437188
  69.8 6.4 %copy-start.2 = (s32[1,96]{1,0:T(1,128)S(1)}, s32[1,96]{1,0:T(1,128)}, u32[]{:S(2)}) copy-start(s32[1,96]{1,0:T(1,128)} %param.12) | copy-start | bytes 1156
  69.8 6.5 %copy-start.3 = (s32[1,96]{1,0:T(1,128)S(1)}, s32[1,96]{1,0:T(1,128)}, u32[]{:S(2)}) copy-start(s32[1,96]{1,0:T(1,128)} %param.13) | copy-start | bytes 1156
  69.8 79.9 %all-to-all-start.1 = ((f32[3,64,8,512]{3,2,0,1:T(8,128)}), f32[3,64,8,512]{3,2,0,1:T(8,128)}, u32[]{:S(2)}, u32[]{:S(2)}) async-start(f32[3,64,8,512]{3,2,0,1:T(8,128)} %copy.17), calls=%async_computation.1 | async-start | bytes 6291456 | tf_op jit(solution)/shard_map/all_to_all | solution.py:45
where the time goes:
time: 239 us; the launch traced here: 238 us
  blocking collectives  129 us (54%)
  waiting for transfers between devices  69.7 us (29%)
  local copies, waits for them, and re-layouts  13.1 us (5%)
  other arithmetic  11.5 us (5%)
  matrix products  8.36 us (3%)
  starting transfers between devices  6.43 us (3%)
    psum x1, blocking collectives, shards(): lax.psum(jnp.sum(direction * direction, axis=(1, 2, 3)), ('fsdp', 'rep'))  76 us
    all_to_all x1, waiting for transfers between devices, shards(): lax.all_to_all(owned_blocks.reshape(owner_slot_count, sharded_data_count,...  69.7 us
    all_to_all x1, blocking collectives, shards(): lax.all_to_all(outbound_blocks, 'fsdp', split_axis=1, concat_axis=1, tile...  52.6 us
    all_to_all x1, starting transfers between devices, shards(): lax.all_to_all(owned_blocks.reshape(owner_slot_count, sharded_data_count,...  6.43 us
    dot_general x1, matrix products, products(): jnp.einsum('sij,sjk->sik', lefts, inner_prod, precision=lax.Precision.HIG...  5.52 us
  transfers between devices with their start and end apart: 1, of which 1 were waited for; matrix products, arithmetic and copies ran while one was open for 2% of the time, Pallas kernels for 0%

commit v1 on v0

v1 whole, which is shorter than its diff:
```python
import functools

import jax
import jax.numpy as jnp
from jax import lax
from jax.experimental import pallas as pl
from jax.experimental.pallas import tpu as pltpu
from jax.sharding import PartitionSpec as P

MESH = pl.DeviceIdType.MESH
NX, NZ, NC, NREP = 4, 8, 2, 4
LINE = NX * NC
SLOTS = 3
B = 512
NBLK = 96
PLACES = LINE * SLOTS
CAP = 24
STEPS = 16.0


def offset_of(k):
    return jnp.where(k % 2 == 1, (k + 1) // 2, (NZ - k // 2) % NZ)


def tables(owner, slot, cap):
    f = lax.axis_index("fsdp")
    x, z, c = f // (NZ * NC), (f // NC) % NZ, f % NC
    blocks = jnp.arange(NBLK, dtype=jnp.int32)
    line = (owner // NC) % NZ
    ox, oc = owner // (NZ * NC), owner % NC
    place = (ox * NC + oc) * SLOTS + slot
    before = (line[None, :] == line[:, None]) & (place[None, :] < place[:, None])
    rank = jnp.sum(before.astype(jnp.int32), axis=1)

    def pick(key, wanted, value):
        return jnp.sum(jnp.where(wanted[:, None] == key[None, :], value[None, :], 0), axis=1)

    line_pos = line * 32 + rank
    dist = jnp.arange(NZ, dtype=jnp.int32)
    pos = jnp.arange(cap, dtype=jnp.int32)
    wanted = (((z + dist) % NZ) * 32)[:, None] + pos[None, :]
    outgoing = pick(line_pos, wanted.reshape(-1), blocks)
    here = line * 32 + place
    j = jnp.arange(LINE, dtype=jnp.int32)
    jx, jc = (x + j // NC) % NX, (c + j % NC) % NC
    jplace = ((jx * NC + jc) * SLOTS)[:, None] + jnp.arange(SLOTS, dtype=jnp.int32)[None, :]
    deal = jnp.minimum(pick(here, z * 32 + jplace.reshape(-1), rank), cap - 1)
    code = (((x - ox) % NX) * NC + (oc + c) % NC) * SLOTS + slot
    collect = pick(line_pos, z * 32 + pos, code)
    mine = pick(here, z * 32 + (x * NC + c) * SLOTS + jnp.arange(SLOTS, dtype=jnp.int32), 1 + blocks // (NBLK // 2))
    over = jnp.max(rank) >= cap
    parts = [outgoing, deal, collect, mine, over.astype(jnp.int32)[None], (z - line) % NZ, jnp.minimum(rank, cap - 1), place]
    offs, at = [], 0
    for part in parts:
        offs.append(at)
        at += part.shape[0]
    return jnp.concatenate(parts).astype(jnp.int32), offs


def kernel(cap, offs, np_groups, tab, g_ref, sm_hbm, mom_hbm, left_hbm, right_hbm,
           mn_hbm, out_hbm, stat_ref,
           gp, sm, mom, mn, lf, rf, lhi, llo, rhi, rlo, thi, tlo, pbuf,
           zout, zin, xout, xin, xrout, xrin, zrout, zrin, zst, xst, nrm, nin, tot,
           lsem, osem, zs, zr, xs, xr, xrs, xrr, zrs, zrr, ns, nr):
    o_out, o_deal, o_col, o_mine, o_over, o_fd, o_fp, o_fe = offs
    f = lax.axis_index("fsdp")
    r = lax.axis_index("rep")
    x, z, c = f // (NZ * NC), (f // NC) % NZ, f % NC
    f32 = jnp.float32

    def zdev(d):
        return (x * (NZ * NC) + lax.rem(z + d, NZ) * NC + c, r)

    def xdev(j):
        return (lax.rem(x + j // NC, NX) * (NZ * NC) + z * NC + lax.rem(c + j % NC, NC), r)

    def rdev(i):
        return (f, lax.rem(r + i, NREP))

    peers = [zdev(d) for d in range(1, NZ)] + [xdev(j) for j in range(1, LINE)] + [rdev(i) for i in range(1, NREP)]
    bar = pltpu.get_barrier_semaphore()
    for dev in peers:
        pl.semaphore_signal(bar, 1, device_id=dev, device_id_type=MESH)

    loads = [
        pltpu.make_async_copy(right_hbm, rf, lsem.at[0]),
        pltpu.make_async_copy(sm_hbm, sm, lsem.at[1]),
        pltpu.make_async_copy(left_hbm, lf, lsem.at[2]),
        pltpu.make_async_copy(mom_hbm, mom, lsem.at[3]),
    ]
    for cp in loads:
        cp.start()

    def repack(i, carry):
        row = g_ref[i].astype(f32)
        for q in range(3):
            a = row[:, q * B:q * B + B // 2]
            b = row[:, q * B + B // 2:(q + 1) * B]
            gp[i * 3 + q] = jnp.concatenate([a, b], axis=0).astype(jnp.bfloat16)
        return carry

    lax.fori_loop(0, 32, repack, 0)

    def fill(d, dst, slot):
        def one(p, carry):
            dst[slot, p] = gp[tab[o_out + d * cap + p]]
            return carry
        lax.fori_loop(0, cap, one, 0, unroll=6)

    def zsend(k, carry):
        d = offset_of(k)
        fill(d, zout, d)

        @pl.when(k == 1)
        def _():
            pl.semaphore_wait(bar, len(peers))

        pltpu.make_async_remote_copy(src_ref=zout.at[d], dst_ref=zin.at[d], send_sem=zs, recv_sem=zr.at[d],
                                     device_id=zdev(d), device_id_type=MESH).start()
        return carry

    lax.fori_loop(1, NZ, zsend, 0)
    fill(0, zin, 0)

    loads[1].wait()

    def adam_m(m):
        def one(k, acc):
            i = m * 16 + k
            g = g_ref[i].astype(f32)
            new = 0.9 * sm[i] + 0.1 * g * g
            mn[i] = new
            a = g / (jnp.sqrt(new) + 1e-8)
            a = a * a
            for q in range(12):
                acc = acc + a[:, q * 128:(q + 1) * 128]
            return acc
        return lax.fori_loop(0, 16, one, jnp.zeros((8, 128), f32))

    adam0 = adam_m(0)
    adam1 = adam_m(1)
    mn_out = pltpu.make_async_copy(mn, mn_hbm, osem.at[0])
    mn_out.start()

    def split(src, hi, lo):
        def one(i, carry):
            for s in range(SLOTS):
                v = src[s, i // NZ, i % NZ]
                h = v.astype(jnp.bfloat16)
                hi[s, i // NZ, i % NZ] = h
                lo[s, i // NZ, i % NZ] = (v - h.astype(f32)).astype(jnp.bfloat16)
            return carry
        lax.fori_loop(0, NX * NZ, one, 0)

    loads[0].wait()
    split(rf, rhi, rlo)
    loads[2].wait()
    split(lf, lhi, llo)
    loads[3].wait()

    def whole(ref, s):
        return ref[s].reshape(B, B)

    def xsend(d):
        zst[...] = zin[d]
        for j in range(LINE):
            for s in range(SLOTS):
                piece = zst[tab[o_deal + j * SLOTS + s]]
                if j:
                    xout[d, j, s] = piece
                else:
                    xin[d, j, s] = piece
            if j:
                pltpu.make_async_remote_copy(src_ref=xout.at[d, j], dst_ref=xin.at[d, j], send_sem=xs,
                                             recv_sem=xr.at[d], device_id=xdev(j), device_id_type=MESH).start()

    def tchunk(d):
        pltpu.make_async_copy(xin.at[d, pl.ds(1, LINE - 1)], xin.at[d, pl.ds(1, LINE - 1)], xr.at[d]).wait()
        zsrc = lax.rem(z - d + NZ, NZ)
        for s in range(SLOTS):
            rows = []
            for dx in range(NX):
                p0 = xin[d, dx * NC + c, s].astype(f32)
                p1 = xin[d, dx * NC + (1 - c), s].astype(f32)
                lft = jnp.concatenate([p0[:8], p1[:8]], axis=0)
                rgt = jnp.concatenate([p0[8:], p1[8:]], axis=0)
                rows.append(jnp.concatenate([lft, rgt], axis=1).astype(jnp.bfloat16))
            a = jnp.concatenate(rows, axis=0)
            t = jnp.dot(a, whole(rhi, s), preferred_element_type=f32) + jnp.dot(a, whole(rlo, s), preferred_element_type=f32)
            h = t.astype(jnp.bfloat16)
            lo = (t - h.astype(f32)).astype(jnp.bfloat16)
            for dx in range(NX):
                xsrc = lax.rem(x - dx + NX, NX)
                thi[s, xsrc, zsrc] = h[dx * 16:(dx + 1) * 16]
                tlo[s, xsrc, zsrc] = lo[dx * 16:(dx + 1) * 16]

    xsend(0)

    def forward(k, carry):
        d = offset_of(k)
        pltpu.make_async_copy(zin.at[d], zin.at[d], zr.at[d]).wait()
        xsend(d)
        tchunk(offset_of(k - 1))
        return carry

    lax.fori_loop(1, NZ, forward, 0)
    tchunk(offset_of(NZ - 1))

    lane = lax.broadcasted_iota(jnp.int32, (8, 128), 1)
    row = lax.broadcasted_iota(jnp.int32, (8, 128), 0)
    base = (x * NC + c) * SLOTS
    nrm[...] = jnp.zeros_like(nrm)
    per = NZ // np_groups

    def pgroup(n):
        for s in range(SLOTS):
            hs, ls = [], []
            for i in range(per):
                zz = lax.rem(z + offset_of((n * per + i + 1) % NZ), NZ)
                hs.append(lhi[s, :, zz].reshape(64, B))
                ls.append(llo[s, :, zz].reshape(64, B))
            h = jnp.concatenate(hs, axis=0)
            lo = jnp.concatenate(ls, axis=0)
            p = jnp.dot(h, whole(thi, s), preferred_element_type=f32)
            p = p + jnp.dot(h, whole(tlo, s), preferred_element_type=f32)
            p = p + jnp.dot(lo, whole(thi, s), preferred_element_type=f32)
            pbuf[s] = p

        def quant(i, carry):
            d = offset_of((n * per + i + 1) % NZ)
            sums = [jnp.zeros((8, 128), f32) for _ in range(SLOTS)]
            for xd in range(NX):
                for cd in range(NC):
                    j = lax.rem(xd - x + NX, NX) * NC + lax.rem(cd + c, NC)
                    lev = jnp.zeros((8, 128), jnp.int32)
                    at = pl.multiple_of(i * 64 + (xd * NC + cd) * 8, 8)
                    for s in range(SLOTS):
                        v = pbuf[s, pl.ds(at, 8), :]
                        sq = v * v
                        sums[s] = sums[s] + ((sq[:, :128] + sq[:, 128:256]) + (sq[:, 256:384] + sq[:, 384:]))
                        top = jnp.maximum(jnp.max(jnp.abs(v), axis=1, keepdims=True), 1e-30)
                        level = jnp.ceil(jnp.log2(top) * STEPS) + 1.0
                        q = jnp.round(v * (jnp.exp2(level * (-1.0 / STEPS)) * 32767.0)).astype(jnp.int32)
                        packed = (q[:, :256] << 16) | (q[:, 256:] & 0xFFFF)
                        xrout[d, j, 2 * s] = packed[:, :128]
                        xrout[d, j, 2 * s + 1] = packed[:, 128:]
                        lev = jnp.where(lane == base + s, level.astype(jnp.int32), lev)
                    xrout[d, j, 2 * SLOTS] = lev
            for s in range(SLOTS):
                which = tab[o_mine + s]
                nrm[0] += jnp.where(which == 1, sums[s], 0.0)
                nrm[1] += jnp.where(which == 2, sums[s], 0.0)
            xrin[d, 0] = xrout[d, 0]
            for j in range(1, LINE):
                pltpu.make_async_remote_copy(src_ref=xrout.at[d, j], dst_ref=xrin.at[d, j], send_sem=xrs,
                                             recv_sem=xrr.at[d], device_id=xdev(j), device_id_type=MESH).start()
            return carry

        lax.fori_loop(0, per, quant, 0)

    def relay(k):
        d = offset_of(k % NZ)
        pltpu.make_async_copy(xrin.at[d, pl.ds(1, LINE - 1)], xrin.at[d, pl.ds(1, LINE - 1)], xrr.at[d]).wait()

        def put(dst):
            for j in range(LINE):
                for s in range(SLOTS):
                    xst[j * SLOTS + s, 0] = xrin[d, j, 2 * s]
                    xst[j * SLOTS + s, 1] = xrin[d, j, 2 * s + 1]

            def one(p, carry):
                code = tab[o_col + p]
                dst[d, 2 * p] = xst[code, 0]
                dst[d, 2 * p + 1] = xst[code, 1]
                return carry
            lax.fori_loop(0, cap, one, 0, unroll=6)
            lev = xrin[d, 0, 2 * SLOTS]
            for j in range(1, LINE):
                lev = lev + xrin[d, j, 2 * SLOTS]
            dst[d, 2 * cap] = lev
        return d, put

    def relay_out(k, carry):
        d, put = relay(k)
        put(zrout)
        pltpu.make_async_remote_copy(src_ref=zrout.at[d], dst_ref=zrin.at[d], send_sem=zrs, recv_sem=zrr.at[d],
                                     device_id=zdev(d), device_id_type=MESH).start()
        return carry

    pgroup(0)

    def back(n, carry):
        pgroup(n)
        lax.fori_loop((n - 1) * per + 1, n * per + 1, relay_out, 0)
        return carry

    if np_groups > 1:
        lax.fori_loop(1, np_groups, back, 0)

    def pack_row(i, v):
        return jnp.where(row == i, jnp.sum(v, axis=0, keepdims=True), 0.0)

    over = jnp.where(tab[o_over] > 0, 1.0, 0.0)
    local = pack_row(0, adam0) + pack_row(1, adam1) + pack_row(2, nrm[0]) + pack_row(3, nrm[1])
    tot[0] = local + jnp.where(row == 4, over, 0.0)

    def share(stage, devs, base_at):
        for i, dev in enumerate(devs):
            pltpu.make_async_remote_copy(src_ref=tot.at[stage], dst_ref=nin.at[base_at + i], send_sem=ns.at[stage],
                                         recv_sem=nr.at[stage], device_id=dev, device_id_type=MESH).start()

    def gather(stage, count, base_at):
        view = nin.at[pl.ds(base_at, count)]
        pltpu.make_async_copy(view, view, nr.at[stage]).wait()
        acc = tot[stage]
        for i in range(count):
            acc = acc + nin[base_at + i]
        return acc

    share(0, [xdev(j) for j in range(1, LINE)], 0)
    lax.fori_loop((np_groups - 1) * per + 1, NZ, relay_out, 0)
    d, put = relay(NZ)
    put(zrin)
    tot[1] = gather(0, LINE - 1, 0)
    share(1, [zdev(d) for d in range(1, NZ)], 7)
    tot[2] = gather(1, NZ - 1, 7)
    share(2, [rdev(i) for i in range(1, NREP)], 14)
    total = gather(2, NREP - 1, 14)
    stat_ref[...] = total
    sums = jnp.sum(total, axis=1, keepdims=True)
    scale = jnp.sqrt(sums[0:2]) / (jnp.sqrt(sums[2:4]) + 1e-6) * (1.0 / 32767.0)

    view = zrin.at[pl.ds(1, NZ - 1)]

    def landed(d, carry):
        pltpu.make_async_copy(zrin.at[d], zrin.at[d], zrr.at[d]).wait()
        return carry

    lax.fori_loop(1, NZ, landed, 0)

    def finish(m):
        factor = scale[m:m + 1]

        def one(k, carry):
            i = m * 16 + k
            for q in range(3):
                b = i * 3 + q
                d, p, e = tab[o_fd + b], tab[o_fp + b], tab[o_fe + b]
                lev = jnp.sum(jnp.where(lane == e, zrin[d, 2 * cap], 0).astype(f32), axis=1, keepdims=True)
                mul = jnp.exp2(lev * (1.0 / STEPS)) * factor
                for h in range(2):
                    w = zrin[d, 2 * p + h]
                    for u, v in ((0, w >> 16), (1, (w << 16) >> 16)):
                        cols = pl.ds(q * B + u * 256 + h * 128, 128)
                        mom[i, :, cols] = 0.9 * mom[i, :, cols] + v.astype(f32) * mul
            return carry

        lax.fori_loop(0, 16, one, 0, unroll=2)
        half = pl.ds(m * 16, 16)
        cp = pltpu.make_async_copy(mom.at[half], out_hbm.at[half], osem.at[1 + m])
        cp.start()
        return cp

    outs = [finish(0), finish(1)]

    def sent(ref, sem):
        pltpu.make_async_copy(ref, ref, sem).wait()

    sent(zout.at[pl.ds(1, NZ - 1)], zs)
    sent(xout.at[:, pl.ds(1, LINE - 1)], xs)
    sent(xrout.at[:, pl.ds(1, LINE - 1)], xrs)
    sent(zrout.at[pl.ds(1, NZ - 1)], zrs)
    sent(nin.at[pl.ds(0, 7)], ns.at[0])
    sent(nin.at[pl.ds(7, 7)], ns.at[1])
    sent(nin.at[pl.ds(14, 3)], ns.at[2])
    mn_out.wait()
    for cp in outs:
        cp.wait()


def fused(grads, second_moment, momentum, left, right, owner, slot, cap, cid):
    table, offs = tables(owner, slot, cap)
    bf16, f32, i32 = jnp.bfloat16, jnp.float32, jnp.int32
    np_groups = 4
    rows = 64 * (NZ // np_groups)
    fac = (SLOTS, NX, NZ, 16, B)
    v, dma = pltpu.VMEM, pltpu.SemaphoreType.DMA
    hbm, vm, sm = (pl.BlockSpec(memory_space=s) for s in (pl.ANY, pltpu.VMEM, pltpu.SMEM))
    flat = (32, 8, 3 * B)
    return pl.pallas_call(
        functools.partial(kernel, cap, offs, np_groups),
        out_shape=(
            jax.ShapeDtypeStruct(flat, f32),
            jax.ShapeDtypeStruct(flat, f32),
            jax.ShapeDtypeStruct((8, 128), f32),
        ),
        in_specs=[sm, vm, hbm, hbm, hbm, hbm],
        out_specs=(hbm, hbm, vm),
        scratch_shapes=[
            v((NBLK, 16, 256), bf16), v(flat, f32), v(flat, f32), v(flat, f32),
            v(fac, f32), v(fac, f32), v(fac, bf16), v(fac, bf16), v(fac, bf16), v(fac, bf16),
            v(fac, bf16), v(fac, bf16), v((SLOTS, rows, B), f32),
            v((NZ, cap, 16, 256), bf16), v((NZ, cap, 16, 256), bf16),
            v((NZ, LINE, SLOTS, 16, 256), bf16), v((NZ, LINE, SLOTS, 16, 256), bf16),
            v((NZ, LINE, 2 * SLOTS + 1, 8, 128), i32), v((NZ, LINE, 2 * SLOTS + 1, 8, 128), i32),
            v((NZ, 2 * cap + 1, 8, 128), i32), v((NZ, 2 * cap + 1, 8, 128), i32),
            v((cap, 16, 256), bf16), v((PLACES, 2, 8, 128), i32),
            v((2, 8, 128), f32), v((17, 8, 128), f32), v((3, 8, 128), f32),
            dma((4,)), dma((3,)), dma, dma((NZ,)), dma, dma((NZ,)), dma, dma((NZ,)), dma, dma((NZ,)),
            dma((3,)), dma((3,)),
        ],
        compiler_params=pltpu.CompilerParams(
            collective_id=cid, has_side_effects=True, vmem_limit_bytes=56 * 2**20
        ),
        cost_estimate=pl.CostEstimate(flops=4 * 10**9, bytes_accessed=14 * 10**6, transcendentals=0),
    )(
        table,
        grads.reshape(flat),
        second_moment.reshape(flat),
        momentum.reshape(flat),
        left.reshape(fac),
        right.reshape(fac),
    )


def shards(grads, second_moment, momentum, left_inverse_root, right_root, owner, slot):
    new, mom, stat = fused(
        grads, second_moment, momentum, left_inverse_root, right_root, owner[0], slot[0], CAP, 0
    )
    return new.reshape(second_moment.shape), mom.reshape(momentum.shape)


def solution(mesh):
    in_specs = (
        P(None, None, "fsdp", "rep"),
        P(None, None, "fsdp", "rep"),
        P(None, None, "fsdp", "rep"),
        P("rep", "fsdp", None, None, None),
        P("rep", "fsdp", None, None, None),
        P("rep", None),
        P("rep", None),
    )
    out_specs = (P(None, None, "fsdp", "rep"), P(None, None, "fsdp", "rep"))
    return jax.shard_map(shards, mesh=mesh, in_specs=in_specs, out_specs=out_specs, check_vma=False)
```

time: 239 us -> 118 us (0.49)
  blocking collectives: 129 us -> 0 us
  Pallas kernels: 0 us -> 108 us
  waiting for transfers between devices: 69.7 us -> 0 us
  matrix products: 8.36 us -> 0 us
  local copies, waits for them, and re-layouts: 13.1 us -> 4.77 us
  other arithmetic: 11.5 us -> 3.85 us
  starting transfers between devices: 6.43 us -> 0 us
    pallas_call x0 -> x1, Pallas kernels: none -> 108 us  [fused(): pl.pallas_call(functools.partial(kernel, cap, offs, np_groups), out_shape...]
    psum x1 -> x0, blocking collectives: 76 us -> none  [shards(): lax.psum(jnp.sum(direction * direction, axis=(1, 2, 3)), ('fsdp', 'rep'))]
    all_to_all x1 -> x0, waiting for transfers between devices: 69.7 us -> none  [shards(): lax.all_to_all(owned_blocks.reshape(owner_slot_count, sharded_data_count,...]
    all_to_all x1 -> x0, blocking collectives: 52.6 us -> none  [shards(): lax.all_to_all(outbound_blocks, 'fsdp', split_axis=1, concat_axis=1, tile...]
    dot_general x2 -> x0, matrix products: 8.36 us -> none  [the longest x1 5.52 us: products(): jnp.einsum('sij,sjk->sik', lefts, inner_prod, precision=lax.Precision.HIG...]
    gather x2 -> x0, local copies, waits for them, and re-layouts: 6.89 us -> none  [the longest x1 3.68 us: shards(): returned_blocks.reshape(owner_slot_count * sharded_data_count, rows_per_s...]
    all_to_all x1 -> x0, starting transfers between devices: 6.43 us -> none  [shards(): lax.all_to_all(owned_blocks.reshape(owner_slot_count, sharded_data_count,...]
    reduce_sum x3 -> x5, other arithmetic: 5.48 us -> 0.92 us  [the longest x4 0.74 us: pick(): jnp.sum(jnp.where(wanted[:, None] == key[None, :], value[None, :], 0), ax...]
  transfers between devices with their start and end apart: 1 -> 0, of which waited for: 1 -> 0; matrix products, arithmetic and copies ran while one was open for 2% -> 0% of each run, Pallas kernels for 0% -> 0%
where the time goes in v1:
time: 118 us
  Pallas kernels  108 us (92%)
  local copies, waits for them, and re-layouts  4.77 us (4%)
  other arithmetic  3.85 us (3%)
  between operations  1.39 us (1%)
    pallas_call x1, Pallas kernels, fused(): pl.pallas_call(functools.partial(kernel, cap, offs, np_groups), out_shape...  108 us
    unnamed x4, local copies, waits for them, and re-layouts  3.92 us

profile of v1, /device:TPU:1, one launch (start us, length us, event | category | flops | bytes accessed | tf_op | source)
XLA Modules:
  0.0 117.9 jit_solution(9079347141230713302)
XLA Ops:
  0.7 0.7 add_bitcast_fusion
  1.4 0.7 and_select_fusion
  2.1 0.7 add_bitcast_fusion.1
  2.8 0.2 select_reduce_fusion.3
  3.0 0.2 convert_reduce_fusion
  3.2 0.2 select_reduce_fusion.1
  3.4 0.6 broadcast_minimum_fusion
  4.7 0.1 add_add_fusion
  4.8 0.1 add.310
  4.8 0.2 select_reduce_fusion.2
  5.0 0.1 iota_add_fusion
  5.1 0.1 add.286
  5.2 0.2 select_reduce_fusion
  5.4 0.7 concatenate.3.tab
  6.1 107.9 %shard_map.86 = (f32[32,8,1536]{2,1,0:T(8,128)}, f32[32,8,1536]{2,1,0:T(8,128)}, f32[8,128]{1,0:T(8,128)}) custom-call(s32[532]{0:T(1024)} %concatenate.3.tab, bf16[32,8,1536]{2,1,0:T(8,128)(2,1)} %bitcast.51, f32[32,8,1536]{2,1,0:T(8,128)} %bitcast.49, f32[32,8,1536]{2,1,0:T(8,128)} %bitcast.50, f32[3,4,8,16,512]{4,3,2,1,0:T(8,128)} %bitcast.47, ...), custom_call_target="tpu_custom_call" | custom-call | flops 4000000000 | bytes 14000000 | tf_op jit(solution)/shard_map/pallas_call | solution.py:390
  114.0 0.0 copy-start
  114.0 2.8 %copy.11 = f32[2,16,8,1536]{3,2,1,0:T(8,128)} copy(f32[2,16,8,1536]{3,2,1,0:T(8,128)} %bitcast.44) | data formatting | bytes 3145728
  116.8 0.0 copy-done
  116.8 1.1 copy.12
  (7 shorter events, 0.1 us)
Async XLA Ops:
  114.0 2.8 %copy-start = (f32[32,8,1536]{2,1,0:T(8,128)S(1)}, f32[32,8,1536]{2,1,0:T(8,128)}, u32[]{:S(2)}) copy-start(f32[32,8,1536]{2,1,0:T(8,128)} %get-tuple-element.5) | copy-start | bytes 4718596

commit v2 on v0

v2 whole, which is shorter than its diff:
```python
import functools

import jax
import jax.numpy as jnp
from jax import lax
from jax.experimental import pallas as pl
from jax.experimental.pallas import tpu as pltpu
from jax.sharding import PartitionSpec as P

MESH = pl.DeviceIdType.MESH
NX, NZ, NC, NREP = 4, 8, 2, 4
LINE = NX * NC
SLOTS = 3
B = 512
NBLK = 96
PLACES = LINE * SLOTS
CAP = 19
GROUPS = 4
LAG_A = 3
LAG_B = 4
ALLP = False
EARLY = 5
FLAT = (32, 8, 1536)
T_DEAL, T_COLLECT, T_MINE, T_FIN = 8, 9, 10, 11
STEPS = 16.0


def offset_of(k):
    return jnp.where(k % 2 == 1, (k + 1) // 2, (NZ - k // 2) % NZ)


def within(i, n):
    return jnp.minimum(jnp.maximum(i, 0), n - 1)


def build_tables(owner, slot, x, z, c, cap):
    i32, f32 = jnp.int32, jnp.float32
    sq = (NBLK, NBLK)
    eye = lax.broadcasted_iota(i32, sq, 0) == lax.broadcasted_iota(i32, sq, 1)

    def column(v):
        wide = jnp.broadcast_to(v.astype(f32), sq)
        return jnp.sum(jnp.where(eye, wide, 0.0), axis=1, keepdims=True)

    line = (owner >> 1) & (NZ - 1)
    ox, oc = owner >> 4, owner & 1
    place = slot * LINE + ox * NC + oc
    linef, placef = line.astype(f32), place.astype(f32)
    line_col, place_col = column(line), column(place)
    before = (jnp.broadcast_to(line_col, sq) == jnp.broadcast_to(linef, sq)) & (
        jnp.broadcast_to(place_col, sq) < jnp.broadcast_to(placef, sq))
    rank = jnp.sum(jnp.where(before, 1.0, 0.0), axis=0, keepdims=True)
    rank_col = column(rank)
    firsts = (jnp.broadcast_to(line_col, sq) == jnp.broadcast_to(linef, sq)) & (
        jnp.broadcast_to(place_col, sq) < float(LINE))
    spare = jnp.maximum(EARLY - jnp.sum(jnp.where(firsts, 1.0, 0.0), axis=0, keepdims=True), 0.0)
    seat = jnp.where((slot == 0) & (rank < float(EARLY)), rank, rank + spare)
    seat_col = column(seat)
    code_col = column(slot * LINE + ((x - ox) & (NX - 1)) * NC + ((oc + c) & 1))
    block_col = lax.broadcasted_iota(i32, (NBLK, 128), 0).astype(f32)
    lane = lax.broadcasted_iota(i32, (NBLK, 128), 1)
    wide = (NBLK, 128)
    line_w, place_w, rank_w, code_w, seat_w = (
        jnp.broadcast_to(v, wide) for v in (line_col, place_col, rank_col, code_col, seat_col))
    lanef = lane.astype(f32)

    def pick(match, value):
        return jnp.sum(jnp.where(match, value, 0.0), axis=0, keepdims=True)

    at_pos = rank_w == lanef
    most = float(NBLK - 1)
    rows = [jnp.minimum(pick(at_pos & (line_w == ((z + d) & (NZ - 1)).astype(f32)), block_col), most) for d in range(NZ)]
    here = line_w == z.astype(f32)
    j = lane & (LINE - 1)
    dealt = ((lane - j) + ((x + (j >> 1)) & (NX - 1)) * NC + ((c + j) & 1)).astype(f32)
    rows.append(jnp.minimum(pick(here & (place_w == dealt), rank_w), cap - 1.0))
    rows.append(jnp.minimum(pick(here & (seat_w == lanef), code_w), PLACES - 1.0))
    mine = (x * NC + c + lane * LINE).astype(f32)
    rows.append(pick(here & (place_w == mine), jnp.where(block_col >= NBLK // 2, 2.0, 1.0)))
    finals = [(z - line) & (NZ - 1), jnp.minimum(seat, cap - 1.0).astype(i32), (ox * NC + oc) * SLOTS + slot]
    top = jnp.max(seat, axis=1, keepdims=True)
    return [r.astype(i32) for r in rows], finals, top


def kernel(cap, per, owner_ref, slot_ref, g_ref, sm_hbm, left_hbm, right_hbm,
           mn_hbm, zr_hbm, stat_ref, tabv,
           tab, gp, sm, mn, lf, rf, lhi, llo, rhi, rlo, thi, tlo, pbuf,
           zout, zin, xout_a, xin_a, xout_b, xin_b, xr_a, xi_a, xr_b, xi_b, zrout, zrin, zst, xst, lev0, nrm, nin, tot,
           lsem, osem, zs, zr_a, zr_b, xs_a, xs_b, xw_a, xw_b, xrs_a, xrs_b, xrw_a, xrw_b, zrs, zrw_a, zrw_b, ns, nr):
    f = lax.axis_index("fsdp")
    r = lax.axis_index("rep")
    x, z, c = f // (NZ * NC), (f // NC) % NZ, f % NC
    f32, bf16 = jnp.float32, jnp.bfloat16

    def zdev(d):
        return (x * (NZ * NC) + lax.rem(z + d, NZ) * NC + c, r)

    def xdev(j):
        return (lax.rem(x + j // NC, NX) * (NZ * NC) + z * NC + lax.rem(c + j % NC, NC), r)

    def rdev(i):
        return (f, lax.rem(r + i, NREP))

    def push(src, dst, ssem, rsem, dev):
        pltpu.make_async_remote_copy(src_ref=src, dst_ref=dst, send_sem=ssem, recv_sem=rsem,
                                     device_id=dev, device_id_type=MESH).start()

    def done(ref, sem):
        pltpu.make_async_copy(ref, ref, sem).wait()

    peers = [zdev(d) for d in range(1, NZ)] + [xdev(j) for j in range(1, LINE)] + [rdev(i) for i in range(1, NREP)]
    bar = pltpu.get_barrier_semaphore()
    for dev in peers:
        pl.semaphore_signal(bar, 1, device_id=dev, device_id_type=MESH)

    loads = [
        pltpu.make_async_copy(right_hbm, rf, lsem.at[0]),
        pltpu.make_async_copy(left_hbm, lf, lsem.at[2]),
        pltpu.make_async_copy(sm_hbm, sm, lsem.at[1]),
    ]
    for cp in loads:
        cp.start()

    rows, finals, top = build_tables(owner_ref[...], slot_ref[...], x, z, c, cap)
    for i, v in enumerate(rows):
        tabv[pl.ds(i, 1), :] = v
    for i, v in enumerate(finals):
        tabv[pl.ds(T_FIN + i, 1), :] = jnp.zeros((1, 128), jnp.int32)
        tabv[pl.ds(T_FIN + i, 1), pl.ds(0, NBLK)] = v
    tabv[pl.ds(T_FIN + 3, 2), :] = jnp.zeros((2, 128), jnp.int32)
    over = jnp.where(top >= cap, 1.0, 0.0)
    tcopy = pltpu.make_async_copy(tabv, tab, lsem.at[3])
    tcopy.start()

    def repack(i, carry):
        row = g_ref[i].astype(f32)
        for q in range(3):
            a = row[:, q * B:q * B + B // 2]
            b = row[:, q * B + B // 2:(q + 1) * B]
            gp[i * 3 + q] = jnp.concatenate([a, b], axis=0).astype(bf16)
        return carry

    lax.fori_loop(0, 32, repack, 0)
    tcopy.wait()

    def fill(d, dst, lo, hi):
        for p in range(lo, hi):
            dst[d, p] = gp[within(tab[d, p], NBLK)]

    part_a, part_b = pl.ds(0, LINE), pl.ds(LINE, cap - LINE)

    def zsend_a(k, carry):
        d = offset_of(k)
        fill(d, zout, 0, LINE)

        @pl.when(k == 1)
        def _():
            pl.semaphore_wait(bar, len(peers))

        push(zout.at[d, part_a], zin.at[d, part_a], zs, zr_a.at[d], zdev(d))
        return carry

    def zsend_b(k, carry):
        d = offset_of(k)
        fill(d, zout, LINE, cap)
        push(zout.at[d, part_b], zin.at[d, part_b], zs, zr_b.at[d], zdev(d))
        return carry

    lax.fori_loop(1, NZ, zsend_a, 0)
    lax.fori_loop(1, NZ, zsend_b, 0)
    fill(0, zin, 0, cap)

    def split(src, hi, lo):
        def one(i, carry):
            for s in range(SLOTS):
                v = src[s, i // NZ, i % NZ]
                h = v.astype(bf16)
                hi[s, i // NZ, i % NZ] = h
                lo[s, i // NZ, i % NZ] = (v - h.astype(f32)).astype(bf16)
            return carry
        lax.fori_loop(0, NX * NZ, one, 0)

    loads[0].wait()
    split(rf, rhi, rlo)
    loads[1].wait()
    split(lf, lhi, llo)

    def whole(ref, s):
        return ref[s].reshape(B, B)

    def tiles(d, s, piece):
        zsrc = lax.rem(z - d + NZ, NZ)
        blocks = []
        for dx in range(NX):
            p0 = piece(dx * NC + c).astype(f32)
            p1 = piece(dx * NC + (1 - c)).astype(f32)
            lft = jnp.concatenate([p0[:8], p1[:8]], axis=0)
            rgt = jnp.concatenate([p0[8:], p1[8:]], axis=0)
            blocks.append(jnp.concatenate([lft, rgt], axis=1).astype(bf16))
        a = jnp.concatenate(blocks, axis=0)
        t = jnp.dot(a, whole(rhi, s), preferred_element_type=f32) + jnp.dot(a, whole(rlo, s), preferred_element_type=f32)
        h = t.astype(bf16)
        lo = (t - h.astype(f32)).astype(bf16)
        for dx in range(NX):
            xsrc = lax.rem(x - dx + NX, NX)
            thi[s, xsrc, zsrc] = h[dx * 16:(dx + 1) * 16]
            tlo[s, xsrc, zsrc] = lo[dx * 16:(dx + 1) * 16]

    others = pl.ds(1, LINE - 1)

    def xsend_a(d):
        zst[pl.ds(0, LINE)] = zin[d, pl.ds(0, LINE)]
        for j in range(LINE):
            piece = zst[within(tab[T_DEAL, j], LINE)]
            if j:
                xout_a[d, j] = piece
                push(xout_a.at[d, j], xin_a.at[d, j], xs_a, xw_a.at[d], xdev(j))
            else:
                xin_a[d, 0] = piece

    def tchunk_a(d):
        done(xin_a.at[d, others], xw_a.at[d])
        tiles(d, 0, lambda j: xin_a[d, j])

    def xsend_b(d):
        zst[...] = zin[d]
        for j in range(LINE):
            for s in (1, 2):
                piece = zst[within(tab[T_DEAL, s * LINE + j], cap)]
                if j:
                    xout_b[d, j, s - 1] = piece
                else:
                    xin_b[d, 0, s - 1] = piece
            if j:
                push(xout_b.at[d, j], xin_b.at[d, j], xs_b, xw_b.at[d], xdev(j))

    def tchunk_b(d):
        done(xin_b.at[d, others], xw_b.at[d])
        for s in (1, 2):
            tiles(d, s, lambda j, s=s: xin_b[d, j, s - 1])

    xsend_a(0)

    def forward_a(k, carry):
        d = offset_of(k)
        done(zin.at[d, part_a], zr_a.at[d])
        xsend_a(d)

        @pl.when(k >= LAG_A)
        def _():
            tchunk_a(offset_of(k - LAG_A))
        return carry

    lax.fori_loop(1, NZ, forward_a, 0)
    lax.fori_loop(NZ - LAG_A, NZ, lambda k, carry: (tchunk_a(offset_of(k)), carry)[1], 0)

    lane = lax.broadcasted_iota(jnp.int32, (8, 128), 1)
    row = lax.broadcasted_iota(jnp.int32, (8, 128), 0)
    base = (x * NC + c) * SLOTS
    nrm[...] = jnp.zeros_like(nrm)

    def back_of(i):
        return offset_of(NZ - 1 - i)

    def product(s, first, count):
        hs, ls = [], []
        for i in range(count):
            zz = lax.rem(z + back_of(first + i), NZ)
            hs.append(lhi[s, :, zz].reshape(64, B))
            ls.append(llo[s, :, zz].reshape(64, B))
        h = jnp.concatenate(hs, axis=0)
        lo = jnp.concatenate(ls, axis=0)
        p = jnp.dot(h, whole(thi, s), preferred_element_type=f32)
        p = p + jnp.dot(h, whole(tlo, s), preferred_element_type=f32)
        return p + jnp.dot(lo, whole(thi, s), preferred_element_type=f32)

    def code_rows(v):
        top = jnp.maximum(jnp.max(jnp.abs(v), axis=1, keepdims=True), 1e-30)
        level = jnp.ceil(jnp.log2(top) * STEPS) + 1.0
        q = jnp.round(v * (jnp.exp2(level * (-1.0 / STEPS)) * 32767.0)).astype(jnp.int32)
        packed = (q[:, :256] << 16) | (q[:, 256:] & 0xFFFF)
        sq = v * v
        return packed, level.astype(jnp.int32), (sq[:, :128] + sq[:, 128:256]) + (sq[:, 256:384] + sq[:, 384:])

    def tally(s, v):
        which = tab[T_MINE, s]
        nrm[0] += jnp.where(which == 1, v, 0.0)
        nrm[1] += jnp.where(which == 2, v, 0.0)

    def target(xd, cd):
        return lax.rem(xd - x + NX, NX) * NC + lax.rem(cd + c, NC)

    pbuf[0] = product(0, 0, NZ)

    def code_a(i, carry):
        d = back_of(i)
        total = jnp.zeros((8, 128), f32)
        for xd in range(NX):
            for cd in range(NC):
                j = target(xd, cd)
                v = pbuf[0, pl.ds(pl.multiple_of(i * 64 + (xd * NC + cd) * 8, 8), 8), :]
                packed, level, sq = code_rows(v)
                total = total + sq
                xr_a[d, j, 0] = packed[:, :128]
                xr_a[d, j, 1] = packed[:, 128:]
                lev0[d, j] = jnp.where(lane == base, level, 0)
        tally(0, total)
        xi_a[d, 0] = xr_a[d, 0]
        for j in range(1, LINE):
            push(xr_a.at[d, j], xi_a.at[d, j], xrs_a, xrw_a.at[d], xdev(j))
        return carry

    lax.fori_loop(0, NZ, code_a, 0)

    loads[2].wait()

    def adam_m(m):
        def one(k, acc):
            i = m * 16 + k
            g = g_ref[i].astype(f32)
            new = 0.9 * sm[i] + 0.1 * g * g
            mn[i] = new
            a = g / (jnp.sqrt(new) + 1e-8)
            a = a * a
            for q in range(12):
                acc = acc + a[:, q * 128:(q + 1) * 128]
            return acc
        return lax.fori_loop(0, 16, one, jnp.zeros((8, 128), f32))

    adam0 = adam_m(0)
    adam1 = adam_m(1)
    mn_out = pltpu.make_async_copy(mn, mn_hbm, osem.at[0])
    mn_out.start()

    seats_a, seats_b = pl.ds(0, 2 * EARLY), pl.ds(2 * EARLY, 2 * (cap - EARLY) + 1)

    def stage_a(d):
        for j in range(LINE):
            xst[j] = xi_a[d, j]

    def seat(dst, d, lo, hi):
        for p in range(lo, hi):
            code = within(tab[T_COLLECT, p], PLACES)
            dst[d, 2 * p] = xst[code, 0]
            dst[d, 2 * p + 1] = xst[code, 1]

    def relay_a(i, dst):
        d = back_of(i)
        done(xi_a.at[d, others], xrw_a.at[d])
        stage_a(d)
        seat(dst, d, 0, EARLY)

    def zback_a(i, carry):
        d = back_of(i)
        push(zrout.at[d, seats_a], zrin.at[d, seats_a], zrs, zrw_a.at[d], zdev(d))
        return carry

    xsend_b(0)

    def forward_b(k, carry):
        d = offset_of(k)
        relay_a(k - 1, zrout)
        done(zin.at[d, part_b], zr_b.at[d])
        xsend_b(d)

        @pl.when(k == NZ - 1)
        def _():
            lax.fori_loop(0, NZ - 1, zback_a, 0)

        @pl.when(k >= LAG_B)
        def _():
            tchunk_b(offset_of(k - LAG_B))
        return carry

    lax.fori_loop(1, NZ, forward_b, 0)
    lax.fori_loop(NZ - LAG_B, NZ, lambda k, carry: (tchunk_b(offset_of(k)), carry)[1], 0)

    def pgroup(n):
        for s in (1, 2):
            pbuf[s, pl.ds(0, 64 * per), :] = product(s, n * per, per)

        def code_b(i, carry):
            d = back_of(n * per + i)
            totals = [jnp.zeros((8, 128), f32) for _ in range(2)]
            for xd in range(NX):
                for cd in range(NC):
                    j = target(xd, cd)
                    lev = lev0[d, j]
                    at = pl.ds(pl.multiple_of(i * 64 + (xd * NC + cd) * 8, 8), 8)
                    for s in (1, 2):
                        packed, level, sq = code_rows(pbuf[s, at, :])
                        totals[s - 1] = totals[s - 1] + sq
                        xr_b[d, j, 2 * s - 2] = packed[:, :128]
                        xr_b[d, j, 2 * s - 1] = packed[:, 128:]
                        lev = jnp.where(lane == base + s, level, lev)
                    xr_b[d, j, 4] = lev
            tally(1, totals[0])
            tally(2, totals[1])
            xi_b[d, 0] = xr_b[d, 0]
            for j in range(1, LINE):
                push(xr_b.at[d, j], xi_b.at[d, j], xrs_b, xrw_b.at[d], xdev(j))
            return carry

        lax.fori_loop(0, per, code_b, 0)

    def relay_b(i, dst):
        d = back_of(i)
        done(xi_b.at[d, others], xrw_b.at[d])
        stage_a(d)
        lev = xi_b[d, 0, 4]
        for j in range(LINE):
            xst[LINE + j] = xi_b[d, j, pl.ds(0, 2)]
            xst[2 * LINE + j] = xi_b[d, j, pl.ds(2, 2)]
            if j:
                lev = lev + xi_b[d, j, 4]
        dst[d, 2 * cap] = lev
        seat(dst, d, EARLY, cap)
        return d

    def relay_out(i, carry):
        d = relay_b(i, zrout)
        push(zrout.at[d, seats_b], zrin.at[d, seats_b], zrs, zrw_b.at[d], zdev(d))
        return carry

    pgroup(0)
    groups = NZ // per

    def back(n, carry):
        pgroup(n)
        if not ALLP:
            lax.fori_loop((n - 1) * per, n * per, relay_out, 0)
        return carry

    lax.fori_loop(1, groups, back, 0)

    def pack_row(i, v):
        return jnp.where(row == i, jnp.sum(v, axis=0, keepdims=True), 0.0)

    local = pack_row(0, adam0) + pack_row(1, adam1) + pack_row(2, nrm[0]) + pack_row(3, nrm[1])
    tot[0] = local + jnp.where(row == 4, over, 0.0)

    def share(stage, devs, base_at):
        for i, dev in enumerate(devs):
            push(tot.at[stage], nin.at[base_at + i], ns.at[stage], nr.at[stage], dev)

    def gather(stage, count, base_at):
        done(nin.at[pl.ds(base_at, count)], nr.at[stage])
        acc = tot[stage]
        for i in range(count):
            acc = acc + nin[base_at + i]
        return acc

    share(0, [xdev(j) for j in range(1, LINE)], 0)
    lax.fori_loop(0 if ALLP else (groups - 1) * per, NZ - 1, relay_out, 0)
    relay_a(NZ - 1, zrin)
    relay_b(NZ - 1, zrin)
    tot[1] = gather(0, LINE - 1, 0)
    share(1, [zdev(d) for d in range(1, NZ)], 7)
    tot[2] = gather(1, NZ - 1, 7)
    share(2, [rdev(i) for i in range(1, NREP)], 14)
    total = gather(2, NREP - 1, 14)
    stat_ref[...] = total

    def landed(d, carry):
        done(zrin.at[d, seats_a], zrw_a.at[d])
        done(zrin.at[d, seats_b], zrw_b.at[d])
        return carry

    lax.fori_loop(1, NZ, landed, 0)
    zr_out = pltpu.make_async_copy(zrin, zr_hbm, osem.at[1])
    zr_out.start()

    done(zout.at[pl.ds(1, NZ - 1)], zs)
    done(xout_a.at[:, others], xs_a)
    done(xout_b.at[:, others], xs_b)
    done(xr_a.at[:, others], xrs_a)
    done(xr_b.at[:, others], xrs_b)
    done(zrout.at[pl.ds(1, NZ - 1)], zrs)
    done(nin.at[pl.ds(0, 7)], ns.at[0])
    done(nin.at[pl.ds(7, 7)], ns.at[1])
    done(nin.at[pl.ds(14, 3)], ns.at[2])
    mn_out.wait()
    zr_out.wait()


def finish(cap, tab, zin, total, mn_hbm, mom_hbm, mn_out, out_hbm, mom, mn, osem, lsem):
    parts = 4
    per = 32 // parts
    loads = []
    for i in range(parts):
        view = pl.ds(i * per, per)
        loads.append(pltpu.make_async_copy(mom_hbm.at[view], mom.at[view], lsem.at[i]))
        loads[-1].start()
    fetch = pltpu.make_async_copy(mn_hbm, mn, lsem.at[parts])
    fetch.start()
    copy = pltpu.make_async_copy(mn, mn_out, osem.at[parts])
    sums = jnp.sum(total[...], axis=1, keepdims=True)
    scale = jnp.sqrt(sums[0:2]) / (jnp.sqrt(sums[2:4]) + 1e-6) * (1.0 / 32767.0)
    lane = lax.broadcasted_iota(jnp.int32, (8, 128), 1)
    outs = []
    for n in range(parts):
        m = n * 2 // parts
        factor = scale[m:m + 1]

        def one(k, carry):
            i = n * per + k
            for q in range(3):
                b = i * 3 + q
                d, p, e = tab[T_FIN, b], tab[T_FIN + 1, b], tab[T_FIN + 2, b]
                lev = jnp.sum(jnp.where(lane == e, zin[d, 2 * cap], 0).astype(jnp.float32), axis=1, keepdims=True)
                mul = jnp.exp2(lev * (1.0 / STEPS)) * factor
                for h in range(2):
                    w = zin[d, 2 * p + h]
                    for u, v in ((0, w >> 16), (1, (w << 16) >> 16)):
                        cols = pl.ds(q * B + u * 256 + h * 128, 128)
                        mom[i, :, cols] = 0.9 * mom[i, :, cols] + v.astype(jnp.float32) * mul
            return carry

        loads[n].wait()
        lax.fori_loop(0, per, one, 0, unroll=4)
        view = pl.ds(n * per, per)
        outs.append(pltpu.make_async_copy(mom.at[view], out_hbm.at[view], osem.at[n]))
        outs[-1].start()
        if n == 0:
            fetch.wait()
            copy.start()
    copy.wait()
    for cp in outs:
        cp.wait()


def spaces():
    return (pl.BlockSpec(memory_space=s) for s in (pl.ANY, pltpu.VMEM, pltpu.SMEM))


def fused(grads, second_moment, left, right, owner, slot, cap, cid):
    bf16, f32, i32 = jnp.bfloat16, jnp.float32, jnp.int32
    fac = (SLOTS, NX, NZ, 16, B)
    v, dma = pltpu.VMEM, pltpu.SemaphoreType.DMA
    hbm, vm, sm = spaces()
    tiles = (NZ, 2 * cap + 1, 8, 128)
    return pl.pallas_call(
        functools.partial(kernel, cap, NZ // GROUPS),
        out_shape=(
            jax.ShapeDtypeStruct(FLAT, f32),
            jax.ShapeDtypeStruct(tiles, i32),
            jax.ShapeDtypeStruct((8, 128), f32),
            jax.ShapeDtypeStruct((16, 128), i32),
        ),
        in_specs=[vm, vm, vm, hbm, hbm, hbm],
        out_specs=(hbm, hbm, vm, vm),
        scratch_shapes=[
            pltpu.SMEM((16, 128), i32),
            v((NBLK, 16, 256), bf16), v(FLAT, f32), v(FLAT, f32),
            v(fac, f32), v(fac, f32), v(fac, bf16), v(fac, bf16), v(fac, bf16), v(fac, bf16),
            v(fac, bf16), v(fac, bf16), v((SLOTS, B, B), f32),
            v((NZ, cap, 16, 256), bf16), v((NZ, cap, 16, 256), bf16),
            v((NZ, LINE, 16, 256), bf16), v((NZ, LINE, 16, 256), bf16),
            v((NZ, LINE, 2, 16, 256), bf16), v((NZ, LINE, 2, 16, 256), bf16),
            v((NZ, LINE, 2, 8, 128), i32), v((NZ, LINE, 2, 8, 128), i32),
            v((NZ, LINE, 5, 8, 128), i32), v((NZ, LINE, 5, 8, 128), i32),
            v(tiles, i32), v(tiles, i32),
            v((cap, 16, 256), bf16), v((PLACES, 2, 8, 128), i32), v((NZ, LINE, 8, 128), i32),
            v((2, 8, 128), f32), v((17, 8, 128), f32), v((3, 8, 128), f32),
            dma((4,)), dma((2,)), dma, dma((NZ,)), dma((NZ,)), dma, dma, dma((NZ,)), dma((NZ,)),
            dma, dma, dma((NZ,)), dma((NZ,)), dma, dma((NZ,)), dma((NZ,)), dma((3,)), dma((3,)),
        ],
        compiler_params=pltpu.CompilerParams(
            collective_id=cid, has_side_effects=True, vmem_limit_bytes=56 * 2**20
        ),
        cost_estimate=pl.CostEstimate(flops=4 * 10**9, bytes_accessed=14 * 10**6, transcendentals=0),
    )(owner, slot, grads.reshape(FLAT), second_moment.reshape(FLAT), left.reshape(fac), right.reshape(fac))


def apply(table, coded, total, new, momentum, cap):
    f32 = jnp.float32
    hbm, vm, sm = spaces()
    dma = pltpu.SemaphoreType.DMA
    out = jax.ShapeDtypeStruct(FLAT, f32)
    return pl.pallas_call(
        functools.partial(finish, cap),
        out_shape=(out, out),
        in_specs=[sm, vm, vm, hbm, hbm],
        out_specs=(hbm, hbm),
        scratch_shapes=[pltpu.VMEM(FLAT, f32), pltpu.VMEM(FLAT, f32), dma((5,)), dma((5,))],
        compiler_params=pltpu.CompilerParams(vmem_limit_bytes=56 * 2**20),
        cost_estimate=pl.CostEstimate(flops=10**6, bytes_accessed=8 * 10**6, transcendentals=0),
    )(table, coded, total, new, momentum.reshape(FLAT))


def general(grads, second_moment, momentum, left, right, owners, slots):
    two, rowblk, rows, width = grads.shape
    colblk = width // B
    g = grads.astype(jnp.float32)
    moment_new = 0.9 * second_moment + 0.1 * g * g
    adam = g / (jnp.sqrt(moment_new) + 1e-08)
    devices = NX * NZ * NC
    pieces = grads.reshape(two, rowblk, rows, colblk, B).transpose(0, 1, 3, 2, 4).reshape(NBLK, rows, B)
    target = slots * devices + owners
    match = target[None, :] == jnp.arange(SLOTS * devices, dtype=jnp.int32)[:, None]
    block_at = jnp.sum(jnp.where(match, jnp.arange(NBLK, dtype=jnp.int32)[None, :], 0), axis=1)
    filled = jnp.any(match, axis=1)
    sent = jnp.where(filled[:, None, None], pieces[block_at], jnp.zeros((), grads.dtype))
    got = lax.all_to_all(sent.reshape(SLOTS, devices, rows, B), "fsdp", split_axis=1, concat_axis=1, tiled=True)
    tile = got.reshape(SLOTS, B, B).astype(jnp.float32)
    full = lax.Precision.HIGHEST
    inner = jnp.einsum("sij,sjk->sik", tile, right[0, 0], precision=full)
    owned = jnp.einsum("sij,sjk->sik", left[0, 0], inner, precision=full)
    back = lax.all_to_all(owned.reshape(SLOTS, devices, rows, B), "fsdp", split_axis=1, concat_axis=1, tiled=True)
    flat = back.reshape(SLOTS * devices, rows, B)[target]
    direction = flat.reshape(two, rowblk, colblk, rows, B).transpose(0, 1, 3, 2, 4).reshape(grads.shape)
    both = jnp.stack([jnp.sum(adam * adam, axis=(1, 2, 3)), jnp.sum(direction * direction, axis=(1, 2, 3))])
    both = lax.psum(both, ("fsdp", "rep"))
    scale = jnp.sqrt(both[0]) / (jnp.sqrt(both[1]) + 1e-06)
    return moment_new.reshape(FLAT), (0.9 * momentum + scale[:, None, None, None] * direction).reshape(FLAT)


def shards(grads, second_moment, momentum, left, right, owner, slot):
    new, coded, total, table = fused(grads, second_moment, left, right, owner, slot, CAP, 0)

    def fast():
        return apply(table, coded, total, new, momentum, CAP)

    def slow():
        return general(grads, second_moment, momentum, left, right, owner[0], slot[0])

    if CAP == PLACES:
        new, mom = fast()
    else:
        new, mom = lax.cond(total[4, 0] > 0.0, slow, fast)
    return new.reshape(second_moment.shape), mom.reshape(momentum.shape)


def solution(mesh):
    in_specs = (
        P(None, None, "fsdp", "rep"),
        P(None, None, "fsdp", "rep"),
        P(None, None, "fsdp", "rep"),
        P("rep", "fsdp", None, None, None),
        P("rep", "fsdp", None, None, None),
        P("rep", None),
        P("rep", None),
    )
    out_specs = (P(None, None, "fsdp", "rep"), P(None, None, "fsdp", "rep"))
    return jax.shard_map(shards, mesh=mesh, in_specs=in_specs, out_specs=out_specs, check_vma=False)
```

time: 239 us -> 93.7 us (0.39)
  blocking collectives: 129 us -> 0 us
  Pallas kernels: 0 us -> 91.3 us
  waiting for transfers between devices: 69.7 us -> 0 us
  local copies, waits for them, and re-layouts: 13.1 us -> 0.53 us
  other arithmetic: 11.5 us -> 0 us
  matrix products: 8.36 us -> 0 us
  starting transfers between devices: 6.43 us -> 0 us
    pallas_call x0 -> x2, Pallas kernels: none -> 91.3 us  [the longest x1 87 us: fused(): pl.pallas_call(functools.partial(kernel, cap, NZ // GROUPS), out_shape=(j...]
    psum x1 -> x0, blocking collectives: 76 us -> none  [shards(): lax.psum(jnp.sum(direction * direction, axis=(1, 2, 3)), ('fsdp', 'rep'))]
    all_to_all x1 -> x0, waiting for transfers between devices: 69.7 us -> none  [shards(): lax.all_to_all(owned_blocks.reshape(owner_slot_count, sharded_data_count,...]
    all_to_all x1 -> x0, blocking collectives: 52.6 us -> none  [shards(): lax.all_to_all(outbound_blocks, 'fsdp', split_axis=1, concat_axis=1, tile...]
    dot_general x2 -> x0, matrix products: 8.36 us -> none  [the longest x1 5.52 us: products(): jnp.einsum('sij,sjk->sik', lefts, inner_prod, precision=lax.Precision.HIG...]
    gather x2 -> x0, local copies, waits for them, and re-layouts: 6.89 us -> none  [the longest x1 3.68 us: shards(): returned_blocks.reshape(owner_slot_count * sharded_data_count, rows_per_s...]
    all_to_all x1 -> x0, starting transfers between devices: 6.43 us -> none  [shards(): lax.all_to_all(owned_blocks.reshape(owner_slot_count, sharded_data_count,...]
    reduce_sum x3 -> x0, other arithmetic: 5.48 us -> none  [the longest x1 3.66 us: shards(): adam_part = jnp.sum(adam * adam, axis=(1, 2, 3))]
  transfers between devices with their start and end apart: 1 -> 0, of which waited for: 1 -> 0; matrix products, arithmetic and copies ran while one was open for 2% -> 0% of each run, Pallas kernels for 0% -> 0%
where the time goes in v2:
time: 93.7 us; the launch traced here: 93.6 us
  Pallas kernels  91.3 us (97%)
  between operations  1.52 us (2%)
    pallas_call x1, Pallas kernels, fused(): pl.pallas_call(functools.partial(kernel, cap, NZ // GROUPS), out_shape=(j...  87 us
    pallas_call x1, Pallas kernels, apply(): pl.pallas_call(functools.partial(finish, cap), out_shape=(out, out), in_s...  4.29 us

profile of v2, /device:TPU:1, one launch (start us, length us, event | category | flops | bytes accessed | tf_op | source)
XLA Modules:
  0.0 93.6 jit_solution(16183189871016228083)
XLA Ops:
  0.6 0.0 copy-start
  0.6 0.0 copy-start.4
  0.6 0.0 copy-start.5
  0.7 87.0 %shard_map.90 = (f32[32,8,1536]{2,1,0:T(8,128)S(1)}, s32[8,39,8,128]{3,2,1,0:T(8,128)S(1)}, f32[8,128]{1,0:T(8,128)S(1)}, s32[16,128]{1,0:T(8,128)S(1)}) custom-call(s32[1,96]{1,0:T(1,128)} %owner_ref.1, s32[1,96]{1,0:T(1,128)} %slot_ref.1, bf16[32,8,1536]{2,1,0:T(8,128)(2,1)} %bitcast.51, f32[32,8,1536]{2,1,0:T(8,128)} %bitcast.56, ...), custom_call_target="tpu_custom_call" | custom-call | flops 4000000000 | bytes 14000000 | tf_op jit(solution)/shard_map/pallas_call | solution.py:542
  87.7 0.5 slice.9
  88.8 0.0 copy-done
  88.8 0.0 copy-done.4
  88.9 0.0 copy-done.5
  88.9 4.5 %conditional.1 = (f32[2,16,8,1536]{3,2,1,0:T(8,128)}, f32[2,16,8,1536]{3,2,1,0:T(8,128)}) conditional(s32[]{:T(128)} %bitcast.29, (f32[2,16,8,1536]{3,2,1,0:T(8,128)}, s32[16,128]{1,0:T(8,128)S(1)}, s32[8,39,8,128]{3,2,1,0:T(8,128)S(1)}, f32[8,128]{1,0:T(8,128)S(1)}, f32[32,8,1536]{2,1,0:T(8,128)S(1)}) %tuple.19, (f32[2,16,8,1536]{3,2,1,0:T(8,128)}, ...), branch_computations={%region_0.0_spmd, %region_1.7_spmd} | conditional | flops 9670063104 | bytes 93602296 | solution.py:630
  88.9 4.3 %branch_0_fun.1 = (f32[32,8,1536]{2,1,0:T(8,128)}, f32[32,8,1536]{2,1,0:T(8,128)}) custom-call(s32[16,128]{1,0:T(8,128)S(1)} %get-tuple-element.28.tab, s32[8,39,8,128]{3,2,1,0:T(8,128)S(1)} %get-tuple-element.29.zin, f32[8,128]{1,0:T(8,128)S(1)} %get-tuple-element.30.total, f32[32,8,1536]{2,1,0:T(8,128)S(1)} %get-tuple-element.31.mn_hbm, ...), custom_call_target="tpu_custom_call" | custom-call | flops 1000000 | bytes 8000000 | tf_op jit(solution)/shard_map/cond/branch_0_fun/pallas_call | solution.py:580
Async XLA Ops:
  0.6 88.2 %copy-start = (bf16[2,16,8,1536]{3,2,1,0:T(8,128)(2,1)S(1)}, bf16[2,16,8,1536]{3,2,1,0:T(8,128)(2,1)}, u32[]{:S(2)}) copy-start(bf16[2,16,8,1536]{3,2,1,0:T(8,128)(2,1)} %param.9) | copy-start | bytes 2359300
  0.6 88.2 %copy-start.4 = (s32[1,96]{1,0:T(1,128)S(1)}, s32[1,96]{1,0:T(1,128)}, u32[]{:S(2)}) copy-start(s32[1,96]{1,0:T(1,128)} %owner_ref.1) | copy-start | bytes 1156
  0.6 88.2 %copy-start.5 = (s32[1,96]{1,0:T(1,128)S(1)}, s32[1,96]{1,0:T(1,128)}, u32[]{:S(2)}) copy-start(s32[1,96]{1,0:T(1,128)} %slot_ref.1) | copy-start | bytes 1156

commit v3 on v1

v3 whole, which is shorter than its diff:
```python
import functools

import jax
import jax.numpy as jnp
from jax import lax
from jax.experimental import pallas as pl
from jax.experimental.pallas import tpu as pltpu
from jax.sharding import PartitionSpec as P

MESH = pl.DeviceIdType.MESH
NX, NZ, NC, NREP = 4, 8, 2, 4
LINE = NX * NC
SLOTS = 3
B = 512
NBLK = 96
PLACES = LINE * SLOTS
CAP = 19
LAG = 3
FIRST = 1
HOP1, HOP2 = 2, 5
FLAT = (32, 8, 1536)
T_DEAL, T_COLLECT, T_MINE, T_FIN = 8, 9, 10, 11
STEPS = 16.0


def offset_of(k):
    return jnp.where(k % 2 == 1, (k + 1) // 2, (NZ - k // 2) % NZ)


def within(i, n):
    return jnp.minimum(jnp.maximum(i, 0), n - 1)


def build_tables(owner, slot, x, z, c, cap):
    i32, f32 = jnp.int32, jnp.float32
    sq = (NBLK, NBLK)
    eye = lax.broadcasted_iota(i32, sq, 0) == lax.broadcasted_iota(i32, sq, 1)

    def column(v):
        wide = jnp.broadcast_to(v.astype(f32), sq)
        return jnp.sum(jnp.where(eye, wide, 0.0), axis=1, keepdims=True)

    line = (owner >> 1) & (NZ - 1)
    ox, oc = owner >> 4, owner & 1
    place = (ox * NC + oc) * SLOTS + slot
    linef, placef = line.astype(f32), place.astype(f32)
    line_col, place_col = column(line), column(place)
    before = (jnp.broadcast_to(line_col, sq) == jnp.broadcast_to(linef, sq)) & (
        jnp.broadcast_to(place_col, sq) < jnp.broadcast_to(placef, sq))
    rank = jnp.sum(jnp.where(before, 1.0, 0.0), axis=0, keepdims=True)
    rank_col = column(rank)
    code_col = column((((x - ox) & (NX - 1)) * NC + ((oc + c) & 1)) * SLOTS + slot)
    block_col = lax.broadcasted_iota(i32, (NBLK, 128), 0).astype(f32)
    lane = lax.broadcasted_iota(i32, (NBLK, 128), 1)
    wide = (NBLK, 128)
    line_w, place_w, rank_w, code_w = (jnp.broadcast_to(v, wide) for v in (line_col, place_col, rank_col, code_col))
    lanef = lane.astype(f32)

    def pick(match, value):
        return jnp.sum(jnp.where(match, value, 0.0), axis=0, keepdims=True)

    at_pos = rank_w == lanef
    rows = [jnp.minimum(pick(at_pos & (line_w == ((z + d) & (NZ - 1)).astype(f32)), block_col), NBLK - 1.0) for d in range(NZ)]
    here = line_w == z.astype(f32)
    j = (lane * 11) >> 5
    s = lane - j * SLOTS
    dealt = ((((x + (j >> 1)) & (NX - 1)) * NC + ((c + j) & 1)) * SLOTS + s).astype(f32)
    rows.append(jnp.minimum(pick(here & (place_w == dealt), rank_w), cap - 1.0))
    rows.append(jnp.minimum(pick(here & at_pos, code_w), PLACES - 1.0))
    mine = ((x * NC + c) * SLOTS + lane).astype(f32)
    rows.append(pick(here & (place_w == mine), jnp.where(block_col >= NBLK // 2, 2.0, 1.0)))
    finals = [(z - line) & (NZ - 1), jnp.minimum(rank, cap - 1.0).astype(i32), place]
    top = jnp.max(rank, axis=1, keepdims=True)
    return [r.astype(i32) for r in rows], finals, top


def kernel(cap, owner_ref, slot_ref, g_ref, sm_hbm, left_hbm, right_hbm,
           mn_hbm, zr_hbm, stat_ref, tabv, flag_ref,
           tab, gp, sm, mn, lf, rf, lhi, llo, rhi, rlo, thi, tlo, pbuf,
           zout, zin, xout, xin, xrout, xrin, zrout, zrin, zst, xst, nrm, nin, tot,
           lsem, osem, zs, zr, xs, xr, xrs, xrr, zrs, zrr, ns, nr):
    f = lax.axis_index("fsdp")
    r = lax.axis_index("rep")
    x, z, c = f // (NZ * NC), (f // NC) % NZ, f % NC
    f32 = jnp.float32

    def zdev(d):
        return (x * (NZ * NC) + lax.rem(z + d, NZ) * NC + c, r)

    def xdev(j):
        return (lax.rem(x + j // NC, NX) * (NZ * NC) + z * NC + lax.rem(c + j % NC, NC), r)

    def rdev(i):
        return (f, lax.rem(r + i, NREP))

    peers = [zdev(d) for d in range(1, NZ)] + [xdev(j) for j in range(1, LINE)] + [rdev(i) for i in range(1, NREP)]
    bar = pltpu.get_barrier_semaphore()
    for dev in peers:
        pl.semaphore_signal(bar, 1, device_id=dev, device_id_type=MESH)

    loads = [
        pltpu.make_async_copy(right_hbm, rf, lsem.at[0]),
        pltpu.make_async_copy(sm_hbm, sm, lsem.at[1]),
        pltpu.make_async_copy(left_hbm, lf, lsem.at[2]),
    ]
    for cp in loads:
        cp.start()

    rows, finals, top = build_tables(owner_ref[...], slot_ref[...], x, z, c, cap)
    for i, v in enumerate(rows):
        tabv[pl.ds(i, 1), :] = v
    for i, v in enumerate(finals):
        tabv[pl.ds(T_FIN + i, 1), :] = jnp.zeros((1, 128), jnp.int32)
        tabv[pl.ds(T_FIN + i, 1), pl.ds(0, NBLK)] = v
    tabv[pl.ds(T_FIN + 3, 2), :] = jnp.zeros((2, 128), jnp.int32)
    over = jnp.where(top >= cap, 1.0, 0.0)
    tcopy = pltpu.make_async_copy(tabv, tab, lsem.at[3])
    tcopy.start()

    def repack(i, carry):
        row = g_ref[i].astype(f32)
        for q in range(3):
            a = row[:, q * B:q * B + B // 2]
            b = row[:, q * B + B // 2:(q + 1) * B]
            gp[i * 3 + q] = jnp.concatenate([a, b], axis=0).astype(jnp.bfloat16)
        return carry

    lax.fori_loop(0, 32, repack, 0)
    tcopy.wait()

    def fill(d, dst, slot):
        def one(p, carry):
            dst[slot, p] = gp[within(tab[d, p], NBLK)]
            return carry
        lax.fori_loop(0, cap, one, 0, unroll=4)

    def zsend(k, carry):
        d = offset_of(k)
        fill(d, zout, d)

        @pl.when(k == 1)
        def _():
            pl.semaphore_wait(bar, len(peers))

        pltpu.make_async_remote_copy(src_ref=zout.at[d], dst_ref=zin.at[d], send_sem=zs, recv_sem=zr.at[d],
                                     device_id=zdev(d), device_id_type=MESH).start()
        return carry

    lax.fori_loop(1, NZ, zsend, 0)
    fill(0, zin, 0)

    loads[1].wait()

    def adam_m(m):
        def one(k, acc):
            i = m * 16 + k
            g = g_ref[i].astype(f32)
            new = 0.9 * sm[i] + 0.1 * g * g
            mn[i] = new
            a = g / (jnp.sqrt(new) + 1e-8)
            a = a * a
            for q in range(12):
                acc = acc + a[:, q * 128:(q + 1) * 128]
            return acc
        return lax.fori_loop(0, 16, one, jnp.zeros((8, 128), f32))

    adam0 = adam_m(0)
    adam1 = adam_m(1)
    mn_out = pltpu.make_async_copy(mn, mn_hbm, osem.at[0])
    mn_out.start()

    def split(src, hi, lo):
        def one(i, carry):
            for s in range(SLOTS):
                v = src[s, i // NZ, i % NZ]
                h = v.astype(jnp.bfloat16)
                hi[s, i // NZ, i % NZ] = h
                lo[s, i // NZ, i % NZ] = (v - h.astype(f32)).astype(jnp.bfloat16)
            return carry
        lax.fori_loop(0, NX * NZ, one, 0)

    loads[0].wait()
    split(rf, rhi, rlo)
    loads[2].wait()
    split(lf, lhi, llo)

    def whole(ref, s):
        return ref[s].reshape(B, B)

    def xsend(d):
        zst[...] = zin[d]
        for j in range(LINE):
            for s in range(SLOTS):
                piece = zst[within(tab[T_DEAL, j * SLOTS + s], cap)]
                if j:
                    xout[d, j, s] = piece
                else:
                    xin[d, j, s] = piece
            if j:
                pltpu.make_async_remote_copy(src_ref=xout.at[d, j], dst_ref=xin.at[d, j], send_sem=xs,
                                             recv_sem=xr.at[d], device_id=xdev(j), device_id_type=MESH).start()

    def tchunk(d):
        pltpu.make_async_copy(xin.at[d, pl.ds(1, LINE - 1)], xin.at[d, pl.ds(1, LINE - 1)], xr.at[d]).wait()
        zsrc = lax.rem(z - d + NZ, NZ)
        for s in range(SLOTS):
            rows = []
            for dx in range(NX):
                p0 = xin[d, dx * NC + c, s].astype(f32)
                p1 = xin[d, dx * NC + (1 - c), s].astype(f32)
                lft = jnp.concatenate([p0[:8], p1[:8]], axis=0)
                rgt = jnp.concatenate([p0[8:], p1[8:]], axis=0)
                rows.append(jnp.concatenate([lft, rgt], axis=1).astype(jnp.bfloat16))
            a = jnp.concatenate(rows, axis=0)
            t = jnp.dot(a, whole(rhi, s), preferred_element_type=f32) + jnp.dot(a, whole(rlo, s), preferred_element_type=f32)
            h = t.astype(jnp.bfloat16)
            lo = (t - h.astype(f32)).astype(jnp.bfloat16)
            for dx in range(NX):
                xsrc = lax.rem(x - dx + NX, NX)
                thi[s, xsrc, zsrc] = h[dx * 16:(dx + 1) * 16]
                tlo[s, xsrc, zsrc] = lo[dx * 16:(dx + 1) * 16]

    xsend(0)

    def forward(k, carry):
        d = offset_of(k)
        pltpu.make_async_copy(zin.at[d], zin.at[d], zr.at[d]).wait()
        xsend(d)

        @pl.when(k >= LAG)
        def _():
            tchunk(offset_of(k - LAG))
        return carry

    lax.fori_loop(1, NZ, forward, 0)
    lax.fori_loop(NZ - LAG, NZ, lambda k, carry: (tchunk(offset_of(k)), carry)[1], 0)

    lane = lax.broadcasted_iota(jnp.int32, (8, 128), 1)
    row = lax.broadcasted_iota(jnp.int32, (8, 128), 0)
    base = (x * NC + c) * SLOTS
    nrm[...] = jnp.zeros_like(nrm)

    def product(first, count):
        for s in range(SLOTS):
            hs, ls = [], []
            for i in range(count):
                zz = lax.rem(z + offset_of(NZ - 1 - (first + i)), NZ)
                hs.append(lhi[s, :, zz].reshape(64, B))
                ls.append(llo[s, :, zz].reshape(64, B))
            h = jnp.concatenate(hs, axis=0)
            lo = jnp.concatenate(ls, axis=0)
            p = jnp.dot(h, whole(thi, s), preferred_element_type=f32)
            p = p + jnp.dot(h, whole(tlo, s), preferred_element_type=f32)
            p = p + jnp.dot(lo, whole(thi, s), preferred_element_type=f32)
            pbuf[s, pl.ds(first * 64, count * 64), :] = p

    def tally(i, carry):
        for s in range(SLOTS):
            acc = jnp.zeros((8, 128), f32)
            for u in range(8):
                v = pbuf[s, pl.ds(pl.multiple_of(i * 64 + u * 8, 8), 8), :]
                sq = v * v
                acc = acc + ((sq[:, :128] + sq[:, 128:256]) + (sq[:, 256:384] + sq[:, 384:]))
            which = tab[T_MINE, s]
            nrm[0] += jnp.where(which == 1, acc, 0.0)
            nrm[1] += jnp.where(which == 2, acc, 0.0)
        return carry

    def encode(i, carry):
        d = offset_of(NZ - 1 - i)
        for xd in range(NX):
            for cd in range(NC):
                j = lax.rem(xd - x + NX, NX) * NC + lax.rem(cd + c, NC)
                lev = jnp.zeros((8, 128), jnp.int32)
                at = pl.multiple_of(i * 64 + (xd * NC + cd) * 8, 8)
                for s in range(SLOTS):
                    v = pbuf[s, pl.ds(at, 8), :]
                    top = jnp.maximum(jnp.max(jnp.abs(v), axis=1, keepdims=True), 1e-30)
                    level = jnp.ceil(jnp.log2(top) * STEPS) + 1.0
                    q = jnp.round(v * (jnp.exp2(level * (-1.0 / STEPS)) * 32767.0)).astype(jnp.int32)
                    packed = (q[:, :256] << 16) | (q[:, 256:] & 0xFFFF)
                    xrout[d, j, 2 * s] = packed[:, :128]
                    xrout[d, j, 2 * s + 1] = packed[:, 128:]
                    lev = jnp.where(lane == base + s, level.astype(jnp.int32), lev)
                xrout[d, j, 2 * SLOTS] = lev
        xrin[d, 0] = xrout[d, 0]
        for j in range(1, LINE):
            pltpu.make_async_remote_copy(src_ref=xrout.at[d, j], dst_ref=xrin.at[d, j], send_sem=xrs,
                                         recv_sem=xrr.at[d], device_id=xdev(j), device_id_type=MESH).start()
        return carry

    def relay(k):
        d = offset_of(NZ - 1 - k)
        pltpu.make_async_copy(xrin.at[d, pl.ds(1, LINE - 1)], xrin.at[d, pl.ds(1, LINE - 1)], xrr.at[d]).wait()

        def put(dst):
            for j in range(LINE):
                for s in range(SLOTS):
                    xst[j * SLOTS + s, 0] = xrin[d, j, 2 * s]
                    xst[j * SLOTS + s, 1] = xrin[d, j, 2 * s + 1]

            def one(p, carry):
                code = within(tab[T_COLLECT, p], PLACES)
                dst[d, 2 * p] = xst[code, 0]
                dst[d, 2 * p + 1] = xst[code, 1]
                return carry
            lax.fori_loop(0, cap, one, 0, unroll=4)
            lev = xrin[d, 0, 2 * SLOTS]
            for j in range(1, LINE):
                lev = lev + xrin[d, j, 2 * SLOTS]
            dst[d, 2 * cap] = lev
        return d, put

    def relay_out(k, carry):
        d, put = relay(k)
        put(zrout)
        pltpu.make_async_remote_copy(src_ref=zrout.at[d], dst_ref=zrin.at[d], send_sem=zrs, recv_sem=zrr.at[d],
                                     device_id=zdev(d), device_id_type=MESH).start()
        return carry

    def pack_row(i, v):
        return jnp.where(row == i, jnp.sum(v, axis=0, keepdims=True), 0.0)

    def share(stage, devs, base_at):
        for i, dev in enumerate(devs):
            pltpu.make_async_remote_copy(src_ref=tot.at[stage], dst_ref=nin.at[base_at + i], send_sem=ns.at[stage],
                                         recv_sem=nr.at[stage], device_id=dev, device_id_type=MESH).start()

    def gather(stage, count, base_at):
        view = nin.at[pl.ds(base_at, count)]
        pltpu.make_async_copy(view, view, nr.at[stage]).wait()
        acc = tot[stage]
        for i in range(count):
            acc = acc + nin[base_at + i]
        return acc

    product(0, FIRST)
    lax.fori_loop(0, FIRST, encode, 0)
    product(FIRST, NZ - FIRST)
    lax.fori_loop(0, NZ, tally, 0)
    local = pack_row(0, adam0) + pack_row(1, adam1) + pack_row(2, nrm[0]) + pack_row(3, nrm[1])
    tot[0] = local + jnp.where(row == 4, over, 0.0)

    share(0, [xdev(j) for j in range(1, LINE)], 0)
    lax.fori_loop(FIRST, NZ, encode, 0)
    lax.fori_loop(0, HOP1, relay_out, 0)
    tot[1] = gather(0, LINE - 1, 0)
    share(1, [zdev(d) for d in range(1, NZ)], 7)
    lax.fori_loop(HOP1, HOP2, relay_out, 0)
    tot[2] = gather(1, NZ - 1, 7)
    share(2, [rdev(i) for i in range(1, NREP)], 14)
    lax.fori_loop(HOP2, NZ - 1, relay_out, 0)
    d, put = relay(NZ - 1)
    put(zrin)
    total = gather(2, NREP - 1, 14)
    stat_ref[...] = total
    flag_ref[0] = (stat_ref[4, 0] > 0.0).astype(jnp.int32)

    def ship(d):
        return pltpu.make_async_copy(zrin.at[d], zr_hbm.at[d], osem.at[1])

    def landed(k, carry):
        d = offset_of(NZ - k)
        pltpu.make_async_copy(zrin.at[d], zrin.at[d], zrr.at[d]).wait()
        ship(d).start()
        return carry

    ship(0).start()
    lax.fori_loop(1, NZ, landed, 0)

    def sent(ref, sem):
        pltpu.make_async_copy(ref, ref, sem).wait()

    sent(zout.at[pl.ds(1, NZ - 1)], zs)
    sent(xout.at[:, pl.ds(1, LINE - 1)], xs)
    sent(xrout.at[:, pl.ds(1, LINE - 1)], xrs)
    sent(zrout.at[pl.ds(1, NZ - 1)], zrs)
    sent(nin.at[pl.ds(0, 7)], ns.at[0])
    sent(nin.at[pl.ds(7, 7)], ns.at[1])
    sent(nin.at[pl.ds(14, 3)], ns.at[2])
    mn_out.wait()
    pltpu.make_async_copy(zrin, zr_hbm, osem.at[1]).wait()


def finish(cap, tab, coded_hbm, total, mn_hbm, mom_hbm, mn_out, out_hbm, zin, mom, mn, osem, lsem):
    parts = 4
    per = 32 // parts
    coded = pltpu.make_async_copy(coded_hbm, zin, lsem.at[parts + 1])
    coded.start()
    loads = []
    for i in range(parts):
        view = pl.ds(i * per, per)
        loads.append(pltpu.make_async_copy(mom_hbm.at[view], mom.at[view], lsem.at[i]))
        loads[-1].start()
    fetch = pltpu.make_async_copy(mn_hbm, mn, lsem.at[parts])
    fetch.start()
    copy = pltpu.make_async_copy(mn, mn_out, osem.at[parts])
    sums = jnp.sum(total[...], axis=1, keepdims=True)
    scale = jnp.sqrt(sums[0:2]) / (jnp.sqrt(sums[2:4]) + 1e-6) * (1.0 / 32767.0)
    lane = lax.broadcasted_iota(jnp.int32, (8, 128), 1)
    outs = []
    coded.wait()
    for n in range(parts):
        m = n * 2 // parts
        factor = scale[m:m + 1]

        def one(k, carry):
            i = n * per + k
            for q in range(3):
                b = i * 3 + q
                d, p, e = tab[T_FIN, b], tab[T_FIN + 1, b], tab[T_FIN + 2, b]
                lev = jnp.sum(jnp.where(lane == e, zin[d, 2 * cap], 0).astype(jnp.float32), axis=1, keepdims=True)
                mul = jnp.exp2(lev * (1.0 / STEPS)) * factor
                for h in range(2):
                    w = zin[d, 2 * p + h]
                    for u, v in ((0, w >> 16), (1, (w << 16) >> 16)):
                        cols = pl.ds(q * B + u * 256 + h * 128, 128)
                        mom[i, :, cols] = 0.9 * mom[i, :, cols] + v.astype(jnp.float32) * mul
            return carry

        loads[n].wait()
        lax.fori_loop(0, per, one, 0, unroll=4)
        view = pl.ds(n * per, per)
        outs.append(pltpu.make_async_copy(mom.at[view], out_hbm.at[view], osem.at[n]))
        outs[-1].start()
        if n == 0:
            fetch.wait()
            copy.start()
    copy.wait()
    for cp in outs:
        cp.wait()


def spaces():
    return (pl.BlockSpec(memory_space=s) for s in (pl.ANY, pltpu.VMEM, pltpu.SMEM))


def fused(grads, second_moment, left, right, owner, slot, cap, cid):
    bf16, f32, i32 = jnp.bfloat16, jnp.float32, jnp.int32
    fac = (SLOTS, NX, NZ, 16, B)
    v, dma = pltpu.VMEM, pltpu.SemaphoreType.DMA
    hbm, vm, sm = spaces()
    tiles = (NZ, 2 * cap + 1, 8, 128)
    return pl.pallas_call(
        functools.partial(kernel, cap),
        out_shape=(
            jax.ShapeDtypeStruct(FLAT, f32),
            jax.ShapeDtypeStruct(tiles, i32),
            jax.ShapeDtypeStruct((8, 128), f32),
            jax.ShapeDtypeStruct((16, 128), i32),
            jax.ShapeDtypeStruct((1,), i32),
        ),
        in_specs=[vm, vm, vm, hbm, hbm, hbm],
        out_specs=(hbm, hbm, vm, vm, sm),
        scratch_shapes=[
            pltpu.SMEM((16, 128), i32),
            v((NBLK, 16, 256), bf16), v(FLAT, f32), v(FLAT, f32),
            v(fac, f32), v(fac, f32), v(fac, bf16), v(fac, bf16), v(fac, bf16), v(fac, bf16),
            v(fac, bf16), v(fac, bf16), v((SLOTS, B, B), f32),
            v((NZ, cap, 16, 256), bf16), v((NZ, cap, 16, 256), bf16),
            v((NZ, LINE, SLOTS, 16, 256), bf16), v((NZ, LINE, SLOTS, 16, 256), bf16),
            v((NZ, LINE, 2 * SLOTS + 1, 8, 128), i32), v((NZ, LINE, 2 * SLOTS + 1, 8, 128), i32),
            v(tiles, i32), v(tiles, i32),
            v((cap, 16, 256), bf16), v((PLACES, 2, 8, 128), i32),
            v((2, 8, 128), f32), v((17, 8, 128), f32), v((3, 8, 128), f32),
            dma((4,)), dma((2,)), dma, dma((NZ,)), dma, dma((NZ,)), dma, dma((NZ,)), dma, dma((NZ,)),
            dma((3,)), dma((3,)),
        ],
        compiler_params=pltpu.CompilerParams(
            collective_id=cid, has_side_effects=True, vmem_limit_bytes=56 * 2**20
        ),
        cost_estimate=pl.CostEstimate(flops=4 * 10**9, bytes_accessed=14 * 10**6, transcendentals=0),
    )(owner, slot, grads.reshape(FLAT), second_moment.reshape(FLAT), left.reshape(fac), right.reshape(fac))


def apply(table, coded, total, new, momentum, cap):
    f32 = jnp.float32
    hbm, vm, sm = spaces()
    dma = pltpu.SemaphoreType.DMA
    out = jax.ShapeDtypeStruct(FLAT, f32)
    return pl.pallas_call(
        functools.partial(finish, cap),
        out_shape=(out, out),
        in_specs=[sm, hbm, vm, hbm, hbm],
        out_specs=(hbm, hbm),
        scratch_shapes=[pltpu.VMEM(coded.shape, coded.dtype), pltpu.VMEM(FLAT, f32), pltpu.VMEM(FLAT, f32), dma((5,)), dma((6,))],
        compiler_params=pltpu.CompilerParams(vmem_limit_bytes=56 * 2**20),
        cost_estimate=pl.CostEstimate(flops=10**6, bytes_accessed=8 * 10**6, transcendentals=0),
    )(table, coded, total, new, momentum.reshape(FLAT))


def general(grads, second_moment, momentum, left, right, owners, slots):
    two, rowblk, rows, width = grads.shape
    colblk = width // B
    g = grads.astype(jnp.float32)
    moment_new = 0.9 * second_moment + 0.1 * g * g
    adam = g / (jnp.sqrt(moment_new) + 1e-08)
    devices = NX * NZ * NC
    pieces = grads.reshape(two, rowblk, rows, colblk, B).transpose(0, 1, 3, 2, 4).reshape(NBLK, rows, B)
    target = slots * devices + owners
    match = target[None, :] == jnp.arange(SLOTS * devices, dtype=jnp.int32)[:, None]
    block_at = jnp.sum(jnp.where(match, jnp.arange(NBLK, dtype=jnp.int32)[None, :], 0), axis=1)
    filled = jnp.any(match, axis=1)
    sent = jnp.where(filled[:, None, None], pieces[block_at], jnp.zeros((), grads.dtype))
    got = lax.all_to_all(sent.reshape(SLOTS, devices, rows, B), "fsdp", split_axis=1, concat_axis=1, tiled=True)
    tile = got.reshape(SLOTS, B, B).astype(jnp.float32)
    full = lax.Precision.HIGHEST
    inner = jnp.einsum("sij,sjk->sik", tile, right[0, 0], precision=full)
    owned = jnp.einsum("sij,sjk->sik", left[0, 0], inner, precision=full)
    back = lax.all_to_all(owned.reshape(SLOTS, devices, rows, B), "fsdp", split_axis=1, concat_axis=1, tiled=True)
    flat = back.reshape(SLOTS * devices, rows, B)[target]
    direction = flat.reshape(two, rowblk, colblk, rows, B).transpose(0, 1, 3, 2, 4).reshape(grads.shape)
    both = jnp.stack([jnp.sum(adam * adam, axis=(1, 2, 3)), jnp.sum(direction * direction, axis=(1, 2, 3))])
    both = lax.psum(both, ("fsdp", "rep"))
    scale = jnp.sqrt(both[0]) / (jnp.sqrt(both[1]) + 1e-06)
    return moment_new.reshape(FLAT), (0.9 * momentum + scale[:, None, None, None] * direction).reshape(FLAT)


def shards(grads, second_moment, momentum, left, right, owner, slot):
    new, coded, total, table, flag = fused(grads, second_moment, left, right, owner, slot, CAP, 0)

    def fast():
        return apply(table, coded, total, new, momentum, CAP)

    def slow():
        return general(grads, second_moment, momentum, left, right, owner[0], slot[0])

    if CAP == PLACES:
        new, mom = fast()
    else:
        new, mom = lax.cond(flag[0] > 0, slow, fast)
    return new.reshape(second_moment.shape), mom.reshape(momentum.shape)


def solution(mesh):
    in_specs = (
        P(None, None, "fsdp", "rep"),
        P(None, None, "fsdp", "rep"),
        P(None, None, "fsdp", "rep"),
        P("rep", "fsdp", None, None, None),
        P("rep", "fsdp", None, None, None),
        P("rep", None),
        P("rep", None),
    )
    out_specs = (P(None, None, "fsdp", "rep"), P(None, None, "fsdp", "rep"))
    return jax.shard_map(shards, mesh=mesh, in_specs=in_specs, out_specs=out_specs, check_vma=False)
```

time: 118 us -> 89.1 us (0.76)
  Pallas kernels: 108 us -> 87.2 us
  local copies, waits for them, and re-layouts: 4.77 us -> 0.01 us
  other arithmetic: 3.85 us -> 0 us
    pallas_call x1 -> x2, Pallas kernels: 108 us -> 87.2 us  [the longest x1 82.5 us: fused(): pl.pallas_call(functools.partial(kernel, cap), out_shape=(jax.ShapeDtypeS...]
    unnamed x4 -> x6, local copies, waits for them, and re-layouts: 3.92 us -> 0.01 us
where the time goes in v3:
time: 89.1 us; the launch traced here: 89 us
  Pallas kernels  87.2 us (98%)
  between operations  1.56 us (2%)
    pallas_call x1, Pallas kernels, fused(): pl.pallas_call(functools.partial(kernel, cap), out_shape=(jax.ShapeDtypeS...  82.5 us
    pallas_call x1, Pallas kernels, apply(): pl.pallas_call(functools.partial(finish, cap), out_shape=(out, out), in_s...  4.66 us

profile of v3, /device:TPU:1, one launch (start us, length us, event | category | flops | bytes accessed | tf_op | source)
XLA Modules:
  0.0 89.0 jit_solution(3987170970416099887)
XLA Ops:
  0.6 0.0 copy-start
  0.6 0.0 copy-start.4
  0.6 0.0 copy-start.5
  0.7 82.5 %shard_map.90 = (f32[32,8,1536]{2,1,0:T(8,128)S(1)}, s32[8,39,8,128]{3,2,1,0:T(8,128)S(1)}, f32[8,128]{1,0:T(8,128)S(1)}, s32[16,128]{1,0:T(8,128)S(1)}, s32[1]{0:T(128)}) custom-call(s32[1,96]{1,0:T(1,128)} %owner_ref.1, s32[1,96]{1,0:T(1,128)} %slot_ref.1, bf16[32,8,1536]{2,1,0:T(8,128)(2,1)} %bitcast.51, f32[32,8,1536]{2,1,0:T(8,128)} %bitcast.56, ...), custom_call_target="tpu_custom_call" | custom-call | flops 4000000000 | bytes 14000000 | tf_op jit(solution)/shard_map/pallas_call | solution.py:444
  83.9 0.0 copy-done
  83.9 0.0 copy-done.4
  83.9 0.0 copy-done.5
  83.9 4.9 %conditional.1 = (f32[2,16,8,1536]{3,2,1,0:T(8,128)}, f32[2,16,8,1536]{3,2,1,0:T(8,128)}) conditional(s32[]{:T(128)} %bitcast.29, (f32[2,16,8,1536]{3,2,1,0:T(8,128)}, s32[16,128]{1,0:T(8,128)S(1)}, s32[8,39,8,128]{3,2,1,0:T(8,128)S(1)}, f32[8,128]{1,0:T(8,128)S(1)}, f32[32,8,1536]{2,1,0:T(8,128)S(1)}) %tuple.19, (f32[2,16,8,1536]{3,2,1,0:T(8,128)}, ...), branch_computations={%region_0.0_spmd, %region_1.7_spmd} | conditional | flops 9670063104 | bytes 93602296 | solution.py:531
  83.9 4.7 %branch_0_fun.1 = (f32[32,8,1536]{2,1,0:T(8,128)}, f32[32,8,1536]{2,1,0:T(8,128)}) custom-call(s32[16,128]{1,0:T(8,128)S(1)} %get-tuple-element.28.tab, s32[8,39,8,128]{3,2,1,0:T(8,128)S(1)} %get-tuple-element.29.coded_hbm, f32[8,128]{1,0:T(8,128)S(1)} %get-tuple-element.30.total, f32[32,8,1536]{2,1,0:T(8,128)S(1)} %get-tuple-element.31.mn_hbm, ...), custom_call_target="tpu_custom_call" | custom-call | flops 1000000 | bytes 8000000 | tf_op jit(solution)/shard_map/cond/branch_0_fun/pallas_call | solution.py:481
Async XLA Ops:
  0.6 83.3 %copy-start = (bf16[2,16,8,1536]{3,2,1,0:T(8,128)(2,1)S(1)}, bf16[2,16,8,1536]{3,2,1,0:T(8,128)(2,1)}, u32[]{:S(2)}) copy-start(bf16[2,16,8,1536]{3,2,1,0:T(8,128)(2,1)} %param.9) | copy-start | bytes 2359300
  0.6 83.3 %copy-start.4 = (s32[1,96]{1,0:T(1,128)S(1)}, s32[1,96]{1,0:T(1,128)}, u32[]{:S(2)}) copy-start(s32[1,96]{1,0:T(1,128)} %owner_ref.1) | copy-start | bytes 1156
  0.6 83.3 %copy-start.5 = (s32[1,96]{1,0:T(1,128)S(1)}, s32[1,96]{1,0:T(1,128)}, u32[]{:S(2)}) copy-start(s32[1,96]{1,0:T(1,128)} %slot_ref.1) | copy-start | bytes 1156

commit v4 on v2

--- a/solution.py
+++ b/solution.py
@@ -15,10 +15,10 @@
 NBLK = 96
 PLACES = LINE * SLOTS
 CAP = 19
-GROUPS = 4
 LAG_A = 3
 LAG_B = 4
-ALLP = False
+FIRST = 1
+HOP1, HOP2 = 2, 5
 EARLY = 5
 FLAT = (32, 8, 1536)
 T_DEAL, T_COLLECT, T_MINE, T_FIN = 8, 9, 10, 11
@@ -82,8 +82,8 @@
     return [r.astype(i32) for r in rows], finals, top
 
 
-def kernel(cap, per, owner_ref, slot_ref, g_ref, sm_hbm, left_hbm, right_hbm,
-           mn_hbm, zr_hbm, stat_ref, tabv,
+def kernel(cap, owner_ref, slot_ref, g_ref, sm_hbm, left_hbm, right_hbm,
+           mn_hbm, zr_hbm, stat_ref, tabv, flag_ref,
            tab, gp, sm, mn, lf, rf, lhi, llo, rhi, rlo, thi, tlo, pbuf,
            zout, zin, xout_a, xin_a, xout_b, xin_b, xr_a, xi_a, xr_b, xi_b, zrout, zrin, zst, xst, lev0, nrm, nin, tot,
            lsem, osem, zs, zr_a, zr_b, xs_a, xs_b, xw_a, xw_b, xrs_a, xrs_b, xrw_a, xrw_b, zrs, zrw_a, zrw_b, ns, nr):
@@ -352,6 +352,7 @@
 
     def zback_a(i, carry):
         d = back_of(i)
+        relay_a(i, zrout)
         push(zrout.at[d, seats_a], zrin.at[d, seats_a], zrs, zrw_a.at[d], zdev(d))
         return carry
 
@@ -359,13 +360,8 @@
 
     def forward_b(k, carry):
         d = offset_of(k)
-        relay_a(k - 1, zrout)
         done(zin.at[d, part_b], zr_b.at[d])
         xsend_b(d)
-
-        @pl.when(k == NZ - 1)
-        def _():
-            lax.fori_loop(0, NZ - 1, zback_a, 0)
 
         @pl.when(k >= LAG_B)
         def _():
@@ -373,35 +369,40 @@
         return carry
 
     lax.fori_loop(1, NZ, forward_b, 0)
+    lax.fori_loop(0, NZ - 1, zback_a, 0)
     lax.fori_loop(NZ - LAG_B, NZ, lambda k, carry: (tchunk_b(offset_of(k)), carry)[1], 0)
 
-    def pgroup(n):
+    def multiply(first, count):
         for s in (1, 2):
-            pbuf[s, pl.ds(0, 64 * per), :] = product(s, n * per, per)
-
-        def code_b(i, carry):
-            d = back_of(n * per + i)
-            totals = [jnp.zeros((8, 128), f32) for _ in range(2)]
-            for xd in range(NX):
-                for cd in range(NC):
-                    j = target(xd, cd)
-                    lev = lev0[d, j]
-                    at = pl.ds(pl.multiple_of(i * 64 + (xd * NC + cd) * 8, 8), 8)
-                    for s in (1, 2):
-                        packed, level, sq = code_rows(pbuf[s, at, :])
-                        totals[s - 1] = totals[s - 1] + sq
-                        xr_b[d, j, 2 * s - 2] = packed[:, :128]
-                        xr_b[d, j, 2 * s - 1] = packed[:, 128:]
-                        lev = jnp.where(lane == base + s, level, lev)
-                    xr_b[d, j, 4] = lev
-            tally(1, totals[0])
-            tally(2, totals[1])
-            xi_b[d, 0] = xr_b[d, 0]
-            for j in range(1, LINE):
-                push(xr_b.at[d, j], xi_b.at[d, j], xrs_b, xrw_b.at[d], xdev(j))
-            return carry
-
-        lax.fori_loop(0, per, code_b, 0)
+            pbuf[s, pl.ds(first * 64, count * 64), :] = product(s, first, count)
+
+    def sums_b(i, carry):
+        for s in (1, 2):
+            acc = jnp.zeros((8, 128), f32)
+            for u in range(8):
+                v = pbuf[s, pl.ds(pl.multiple_of(i * 64 + u * 8, 8), 8), :]
+                sq = v * v
+                acc = acc + ((sq[:, :128] + sq[:, 128:256]) + (sq[:, 256:384] + sq[:, 384:]))
+            tally(s, acc)
+        return carry
+
+    def code_b(i, carry):
+        d = back_of(i)
+        for xd in range(NX):
+            for cd in range(NC):
+                j = target(xd, cd)
+                lev = lev0[d, j]
+                at = pl.ds(pl.multiple_of(i * 64 + (xd * NC + cd) * 8, 8), 8)
+                for s in (1, 2):
+                    packed, level, _ = code_rows(pbuf[s, at, :])
+                    xr_b[d, j, 2 * s - 2] = packed[:, :128]
+                    xr_b[d, j, 2 * s - 1] = packed[:, 128:]
+                    lev = jnp.where(lane == base + s, level, lev)
+                xr_b[d, j, 4] = lev
+        xi_b[d, 0] = xr_b[d, 0]
+        for j in range(1, LINE):
+            push(xr_b.at[d, j], xi_b.at[d, j], xrs_b, xrw_b.at[d], xdev(j))
+        return carry
 
     def relay_b(i, dst):
         d = back_of(i)
@@ -422,22 +423,8 @@
         push(zrout.at[d, seats_b], zrin.at[d, seats_b], zrs, zrw_b.at[d], zdev(d))
         return carry
 
-    pgroup(0)
-    groups = NZ // per
-
-    def back(n, carry):
-        pgroup(n)
-        if not ALLP:
-            lax.fori_loop((n - 1) * per, n * per, relay_out, 0)
-        return carry
-
-    lax.fori_loop(1, groups, back, 0)
-
     def pack_row(i, v):
         return jnp.where(row == i, jnp.sum(v, axis=0, keepdims=True), 0.0)
-
-    local = pack_row(0, adam0) + pack_row(1, adam1) + pack_row(2, nrm[0]) + pack_row(3, nrm[1])
-    tot[0] = local + jnp.where(row == 4, over, 0.0)
 
     def share(stage, devs, base_at):
         for i, dev in enumerate(devs):
@@ -450,25 +437,40 @@
             acc = acc + nin[base_at + i]
         return acc
 
+    multiply(0, FIRST)
+    lax.fori_loop(0, FIRST, code_b, 0)
+    multiply(FIRST, NZ - FIRST)
+    lax.fori_loop(0, NZ, sums_b, 0)
+    local = pack_row(0, adam0) + pack_row(1, adam1) + pack_row(2, nrm[0]) + pack_row(3, nrm[1])
+    tot[0] = local + jnp.where(row == 4, over, 0.0)
+
     share(0, [xdev(j) for j in range(1, LINE)], 0)
-    lax.fori_loop(0 if ALLP else (groups - 1) * per, NZ - 1, relay_out, 0)
+    lax.fori_loop(FIRST, NZ, code_b, 0)
+    lax.fori_loop(0, HOP1, relay_out, 0)
+    tot[1] = gather(0, LINE - 1, 0)
+    share(1, [zdev(d) for d in range(1, NZ)], 7)
+    lax.fori_loop(HOP1, HOP2, relay_out, 0)
+    tot[2] = gather(1, NZ - 1, 7)
+    share(2, [rdev(i) for i in range(1, NREP)], 14)
+    lax.fori_loop(HOP2, NZ - 1, relay_out, 0)
     relay_a(NZ - 1, zrin)
     relay_b(NZ - 1, zrin)
-    tot[1] = gather(0, LINE - 1, 0)
-    share(1, [zdev(d) for d in range(1, NZ)], 7)
-    tot[2] = gather(1, NZ - 1, 7)
-    share(2, [rdev(i) for i in range(1, NREP)], 14)
     total = gather(2, NREP - 1, 14)
     stat_ref[...] = total
-
-    def landed(d, carry):
+    flag_ref[0] = (stat_ref[4, 0] > 0.0).astype(jnp.int32)
+
+    def ship(d):
+        return pltpu.make_async_copy(zrin.at[d], zr_hbm.at[d], osem.at[1 + d])
+
+    def landed(k, carry):
+        d = offset_of(NZ - k)
         done(zrin.at[d, seats_a], zrw_a.at[d])
         done(zrin.at[d, seats_b], zrw_b.at[d])
-        return carry
-
+        ship(d).start()
+        return carry
+
+    ship(0).start()
     lax.fori_loop(1, NZ, landed, 0)
-    zr_out = pltpu.make_async_copy(zrin, zr_hbm, osem.at[1])
-    zr_out.start()
 
     done(zout.at[pl.ds(1, NZ - 1)], zs)
     done(xout_a.at[:, others], xs_a)
@@ -480,12 +482,15 @@
     done(nin.at[pl.ds(7, 7)], ns.at[1])
     done(nin.at[pl.ds(14, 3)], ns.at[2])
     mn_out.wait()
-    zr_out.wait()
-
-
-def finish(cap, tab, zin, total, mn_hbm, mom_hbm, mn_out, out_hbm, mom, mn, osem, lsem):
+    for d in range(NZ):
+        ship(d).wait()
+
+
+def finish(cap, tab, coded_hbm, total, mn_hbm, mom_hbm, mn_out, out_hbm, zin, mom, mn, osem, lsem):
     parts = 4
     per = 32 // parts
+    coded = pltpu.make_async_copy(coded_hbm, zin, lsem.at[parts + 1])
+    coded.start()
     loads = []
     for i in range(parts):
         view = pl.ds(i * per, per)
@@ -498,6 +503,7 @@
     scale = jnp.sqrt(sums[0:2]) / (jnp.sqrt(sums[2:4]) + 1e-6) * (1.0 / 32767.0)
     lane = lax.broadcasted_iota(jnp.int32, (8, 128), 1)
     outs = []
+    coded.wait()
     for n in range(parts):
         m = n * 2 // parts
         factor = scale[m:m + 1]
@@ -540,15 +546,16 @@
     hbm, vm, sm = spaces()
     tiles = (NZ, 2 * cap + 1, 8, 128)
     return pl.pallas_call(
-        functools.partial(kernel, cap, NZ // GROUPS),
+        functools.partial(kernel, cap),
         out_shape=(
             jax.ShapeDtypeStruct(FLAT, f32),
             jax.ShapeDtypeStruct(tiles, i32),
             jax.ShapeDtypeStruct((8, 128), f32),
             jax.ShapeDtypeStruct((16, 128), i32),
+            jax.ShapeDtypeStruct((1,), i32),
         ),
         in_specs=[vm, vm, vm, hbm, hbm, hbm],
-        out_specs=(hbm, hbm, vm, vm),
+        out_specs=(hbm, hbm, vm, vm, sm),
         scratch_shapes=[
             pltpu.SMEM((16, 128), i32),
             v((NBLK, 16, 256), bf16), v(FLAT, f32), v(FLAT, f32),
@@ -562,7 +569,7 @@
             v(tiles, i32), v(tiles, i32),
             v((cap, 16, 256), bf16), v((PLACES, 2, 8, 128), i32), v((NZ, LINE, 8, 128), i32),
             v((2, 8, 128), f32), v((17, 8, 128), f32), v((3, 8, 128), f32),
-            dma((4,)), dma((2,)), dma, dma((NZ,)), dma((NZ,)), dma, dma, dma((NZ,)), dma((NZ,)),
+            dma((4,)), dma((1 + NZ,)), dma, dma((NZ,)), dma((NZ,)), dma, dma, dma((NZ,)), dma((NZ,)),
             dma, dma, dma((NZ,)), dma((NZ,)), dma, dma((NZ,)), dma((NZ,)), dma((3,)), dma((3,)),
         ],
         compiler_params=pltpu.CompilerParams(
@@ -580,9 +587,9 @@
     return pl.pallas_call(
         functools.partial(finish, cap),
         out_shape=(out, out),
-        in_specs=[sm, vm, vm, hbm, hbm],
+        in_specs=[sm, hbm, vm, hbm, hbm],
         out_specs=(hbm, hbm),
-        scratch_shapes=[pltpu.VMEM(FLAT, f32), pltpu.VMEM(FLAT, f32), dma((5,)), dma((5,))],
+        scratch_shapes=[pltpu.VMEM(coded.shape, coded.dtype), pltpu.VMEM(FLAT, f32), pltpu.VMEM(FLAT, f32), dma((5,)), dma((6,))],
         compiler_params=pltpu.CompilerParams(vmem_limit_bytes=56 * 2**20),
         cost_estimate=pl.CostEstimate(flops=10**6, bytes_accessed=8 * 10**6, transcendentals=0),
     )(table, coded, total, new, momentum.reshape(FLAT))
@@ -616,7 +623,7 @@
 
 
 def shards(grads, second_moment, momentum, left, right, owner, slot):
-    new, coded, total, table = fused(grads, second_moment, left, right, owner, slot, CAP, 0)
+    new, coded, total, table, flag = fused(grads, second_moment, left, right, owner, slot, CAP, 0)
 
     def fast():
         return apply(table, coded, total, new, momentum, CAP)
@@ -627,7 +634,7 @@
     if CAP == PLACES:
         new, mom = fast()
     else:
-        new, mom = lax.cond(total[4, 0] > 0.0, slow, fast)
+        new, mom = lax.cond(flag[0] > 0, slow, fast)
     return new.reshape(second_moment.shape), mom.reshape(momentum.shape)
 
 

time: 93.7 us -> 89 us (0.950)
  Pallas kernels: 91.3 us -> 87 us
    pallas_call x1, Pallas kernels: 87 us -> 82.4 us  [fused(): pl.pallas_call(functools.partial(kernel, cap), out_shape=(jax.ShapeDtypeS...]
where the time goes in v4:
time: 89 us; the launch traced here: 88.8 us
  Pallas kernels  87 us (98%)
  between operations  1.56 us (2%)
    pallas_call x1, Pallas kernels, fused(): pl.pallas_call(functools.partial(kernel, cap), out_shape=(jax.ShapeDtypeS...  82.4 us
    pallas_call x1, Pallas kernels, apply(): pl.pallas_call(functools.partial(finish, cap), out_shape=(out, out), in_s...  4.66 us

profile of v4, /device:TPU:1, one launch (start us, length us, event | category | flops | bytes accessed | tf_op | source)
XLA Modules:
  0.0 88.8 jit_solution(11695202844347631976)
XLA Ops:
  0.6 0.0 copy-start
  0.6 0.0 copy-start.4
  0.6 0.0 copy-start.5
  0.7 82.4 %shard_map.90 = (f32[32,8,1536]{2,1,0:T(8,128)S(1)}, s32[8,39,8,128]{3,2,1,0:T(8,128)S(1)}, f32[8,128]{1,0:T(8,128)S(1)}, s32[16,128]{1,0:T(8,128)S(1)}, s32[1]{0:T(128)}) custom-call(s32[1,96]{1,0:T(1,128)} %owner_ref.1, s32[1,96]{1,0:T(1,128)} %slot_ref.1, bf16[32,8,1536]{2,1,0:T(8,128)(2,1)} %bitcast.51, f32[32,8,1536]{2,1,0:T(8,128)} %bitcast.56, ...), custom_call_target="tpu_custom_call" | custom-call | flops 4000000000 | bytes 14000000 | tf_op jit(solution)/shard_map/pallas_call | solution.py:548
  83.7 0.0 copy-done
  83.7 0.0 copy-done.4
  83.7 0.0 copy-done.5
  83.7 4.9 %conditional.1 = (f32[2,16,8,1536]{3,2,1,0:T(8,128)}, f32[2,16,8,1536]{3,2,1,0:T(8,128)}) conditional(s32[]{:T(128)} %bitcast.29, (f32[2,16,8,1536]{3,2,1,0:T(8,128)}, s32[16,128]{1,0:T(8,128)S(1)}, s32[8,39,8,128]{3,2,1,0:T(8,128)S(1)}, f32[8,128]{1,0:T(8,128)S(1)}, f32[32,8,1536]{2,1,0:T(8,128)S(1)}) %tuple.19, (f32[2,16,8,1536]{3,2,1,0:T(8,128)}, ...), branch_computations={%region_0.0_spmd, %region_1.7_spmd} | conditional | flops 9670063104 | bytes 93602296 | solution.py:637
  83.8 4.7 %branch_0_fun.1 = (f32[32,8,1536]{2,1,0:T(8,128)}, f32[32,8,1536]{2,1,0:T(8,128)}) custom-call(s32[16,128]{1,0:T(8,128)S(1)} %get-tuple-element.28.tab, s32[8,39,8,128]{3,2,1,0:T(8,128)S(1)} %get-tuple-element.29.coded_hbm, f32[8,128]{1,0:T(8,128)S(1)} %get-tuple-element.30.total, f32[32,8,1536]{2,1,0:T(8,128)S(1)} %get-tuple-element.31.mn_hbm, ...), custom_call_target="tpu_custom_call" | custom-call | flops 1000000 | bytes 8000000 | tf_op jit(solution)/shard_map/cond/branch_0_fun/pallas_call | solution.py:587
Async XLA Ops:
  0.6 83.1 %copy-start = (bf16[2,16,8,1536]{3,2,1,0:T(8,128)(2,1)S(1)}, bf16[2,16,8,1536]{3,2,1,0:T(8,128)(2,1)}, u32[]{:S(2)}) copy-start(bf16[2,16,8,1536]{3,2,1,0:T(8,128)(2,1)} %param.9) | copy-start | bytes 2359300
  0.6 83.1 %copy-start.4 = (s32[1,96]{1,0:T(1,128)S(1)}, s32[1,96]{1,0:T(1,128)}, u32[]{:S(2)}) copy-start(s32[1,96]{1,0:T(1,128)} %owner_ref.1) | copy-start | bytes 1156
  0.6 83.1 %copy-start.5 = (s32[1,96]{1,0:T(1,128)S(1)}, s32[1,96]{1,0:T(1,128)}, u32[]{:S(2)}) copy-start(s32[1,96]{1,0:T(1,128)} %slot_ref.1) | copy-start | bytes 1156
